TPU v7x, 32 devices: a whole 2x2x4 slice. The times are simulated.
32 devices in a mesh: dp: 2 (over core), blk: 16 (over z, y, x).
Axes of the slice: x: 2, y: 2, z: 4, core: 2. Of those that a mesh axis runs over, the one named last changes fastest.
Arguments:
- tokens: bfloat16 [8, 2048, 512], P('dp', 'blk'), may hold values from -6 to 6
- attn_gain: float32 [2, 512], replicated, may hold values from 0.5 to 1.5
- attn_bias: float32 [2, 512], replicated, may hold values from -1.25 to 1.25
- w_qkv: bfloat16 [2, 512, 1536], replicated, may hold values from -0.375 to 0.375
- w_out: bfloat16 [2, 512, 512], replicated, may hold values from -2 to 2
- b_out: float32 [2, 512], replicated, may hold values from -1.25 to 1.25
- mlp_gain: float32 [512], replicated, may hold values from 0.5 to 1.5
- mlp_bias: float32 [512], replicated, may hold values from -1.25 to 1.25
- w_up: bfloat16 [512, 2048], replicated, may hold values from -0.25 to 0.25
- b_up: float32 [2048], replicated, may hold values from -1.25 to 1.25
- w_down: bfloat16 [2048, 512], replicated, may hold values from -0.1875 to 0.1875
- b_down: float32 [512], replicated, may hold values from -1.25 to 1.25
- moe_gain: float32 [512], replicated, may hold values from 0.5 to 1.5
- moe_bias: float32 [512], replicated, may hold values from -1.25 to 1.25
- router: bfloat16 [512, 16], replicated, may hold values from -0.1875 to 0.1875
- expert_up: bfloat16 [16, 512, 2048], P('blk'), may hold values from -0.25 to 0.25
- expert_up_bias: float32 [16, 2048], P('blk'), may hold values from -1.25 to 1.25
- expert_down: bfloat16 [16, 2048, 512], P('blk'), may hold values from -3 to 3
- expert_down_bias: float32 [16, 512], P('blk'), may hold values from -6 to 6
- priority: int32 [32, 512], P(('dp', 'blk')), may hold values from 0 to 511, each once within a row
- routes: int32 [8, 2048, 2], P('dp', 'blk'), may hold values from 0 to 15, all different within a row
- out_grad: bfloat16 [8, 2048, 512], P('dp', 'blk'), may hold values from -6 to 6
Outputs:
- result: bfloat16 [8, 2048, 512], P('dp', 'blk')
- tokens_grad: float32 [8, 2048, 512], P('dp', 'blk')
- attn_gain_grad: float32 [2, 512], replicated
- attn_bias_grad: float32 [2, 512], replicated
- w_qkv_grad: float32 [2, 512, 1536], replicated
- w_out_grad: float32 [2, 512, 512], replicated
- b_out_grad: float32 [2, 512], replicated
- mlp_gain_grad: float32 [512], replicated
- mlp_bias_grad: float32 [512], replicated
- w_up_grad: float32 [512, 2048], replicated
- b_up_grad: float32 [2048], replicated
- w_down_grad: float32 [2048, 512], replicated
- b_down_grad: float32 [512], replicated
- moe_gain_grad: float32 [512], replicated
- moe_bias_grad: float32 [512], replicated
- router_grad: float32 [512, 16], replicated
- expert_up_grad: float32 [16, 512, 2048], P('blk', 'dp')
- expert_up_bias_grad: float32 [16, 2048], P('blk', 'dp')
- expert_down_grad: float32 [16, 2048, 512], P('blk', 'dp')
- expert_down_bias_grad: float32 [16, 512], P('blk', 'dp')
- kept_count: int32 [16], replicated
- dropped_count: int32 [16], replicated
Inputs may be any that keep to these rules, and one draw needn't show every extreme that they name: `priority`: each row is a permutation: the ranks of one routing group's tokens, image-major. `routes`: the two experts of a patch differ.
All inputs are finite; a program needn't handle non-finite values.
Results may differ from a plain program's by a relative error of at most 0.019.
Values may be sent and summed in bfloat16 or wider, within the bound.
No kernel may reach another device: no remote copies, remote signals or barrier semaphores. Data moves between devices by JAX's collectives and lax.ppermute only.
A program may use at most 192 MiB of HBM per device.

v0:
```python
import jax
import jax.numpy as jnp
from jax import lax
from jax.sharding import PartitionSpec as P

HEADS = 8


epsilon = 1e-06


def layer_norm(stream, norm_gain, norm_bias):
    centre = jnp.mean(stream, axis=-1, keepdims=True)
    shifted = stream - centre
    spread = jnp.mean(shifted * shifted, axis=-1, keepdims=True)
    return shifted * lax.rsqrt(spread + epsilon) * norm_gain + norm_bias


def softmax_rows(logits):
    largest = jnp.max(logits, axis=-1, keepdims=True)
    weights = jnp.exp(logits - largest)
    return weights / jnp.sum(weights, axis=-1, keepdims=True)


def gelu_exact(values):
    return jax.nn.gelu(values, approximate=False)


def place_slots(ranking, choices, experts, capacity):
    tok_count = ranking.shape[0]
    order = (
        jnp.zeros((tok_count,), jnp.int32).at[ranking].set(jnp.arange(tok_count, dtype=jnp.int32))
    )
    ordered = choices[order]
    labels = jnp.arange(experts, dtype=jnp.int32)
    first = (ordered[:, 0:1] == labels[None, :]).astype(jnp.int32)
    second = (ordered[:, 1:2] == labels[None, :]).astype(jnp.int32)
    first_before = jnp.cumsum(first, axis=0) - first
    second_before = jnp.cumsum(second, axis=0) - second + jnp.sum(first, axis=0, keepdims=True)
    first_place = jnp.sum(first_before * first, axis=1)
    second_place = jnp.sum(second_before * second, axis=1)
    position = jnp.stack([first_place, second_place], axis=1)[ranking]
    kept = position < capacity
    places = jnp.where(kept, choices * capacity + position, experts * capacity - 1)
    kept_int = kept.astype(jnp.int32)
    matches = (choices[:, :, None] == labels[None, None, :]).astype(jnp.int32)
    kept_hits = jnp.sum(matches * kept_int[:, :, None], axis=(0, 1))
    dropped_hits = jnp.sum(matches, axis=(0, 1)) - kept_hits
    return (places, kept.astype(jnp.float32), kept_hits, dropped_hits)


def to_heads(flat, images, patches, columns):
    return (
        flat.reshape(images, patches, HEADS, columns)
        .transpose(0, 2, 1, 3)
        .reshape(images * HEADS, patches, columns)
    )


def from_heads(stacked, images, patches, columns):
    return (
        stacked.reshape(images, HEADS, patches, columns)
        .transpose(0, 2, 1, 3)
        .reshape(images * patches, HEADS * columns)
    )


def local_attention(queries, key_heads, value_heads):
    pair_count, length, head_size = queries.shape
    row_block = min(512, length)
    query_blocks = queries.reshape(pair_count, length // row_block, row_block, head_size).transpose(
        1, 0, 2, 3
    )

    def one_block(query_block):
        scores = (
            jnp.einsum("pqc,pkc->pqk", query_block, key_heads, preferred_element_type=jnp.float32)
            * 0.125
        )
        largest = jnp.max(scores, axis=-1, keepdims=True)
        weights = jnp.exp(scores - largest)
        totals = jnp.sum(weights, axis=-1, keepdims=True)
        rounded = (weights / totals).astype(jnp.bfloat16)
        output = jnp.einsum(
            "pqk,pkc->pqc", rounded, value_heads, preferred_element_type=jnp.float32
        )
        return (output, (largest + jnp.log(totals))[..., 0])

    outputs, log_sums = lax.map(one_block, query_blocks)
    outputs = outputs.transpose(1, 0, 2, 3).reshape(pair_count, length, head_size)
    log_sums = log_sums.transpose(1, 0, 2).reshape(pair_count, length)
    return (outputs, log_sums)


def local_attention_back(queries, key_heads, value_heads, log_sums, out_grads):
    pair_count, length, head_size = queries.shape
    row_block = min(512, length)
    splits = length // row_block
    query_blocks = queries.reshape(pair_count, splits, row_block, head_size).transpose(1, 0, 2, 3)
    sum_blocks = log_sums.reshape(pair_count, splits, row_block).transpose(1, 0, 2)
    grad_blocks = out_grads.reshape(pair_count, splits, row_block, head_size).transpose(1, 0, 2, 3)

    def one_block(running, pieces):
        key_grad, value_grad = running
        query_block, sum_block, grad_block = pieces
        scores = (
            jnp.einsum("pqc,pkc->pqk", query_block, key_heads, preferred_element_type=jnp.float32)
            * 0.125
        )
        weights = jnp.exp(scores - sum_block[..., None])
        weight_grad = jnp.einsum(
            "pqc,pkc->pqk", grad_block, value_heads, preferred_element_type=jnp.float32
        )
        row_dot = jnp.sum(weight_grad * weights, axis=-1, keepdims=True)
        score_grad = (weights * (weight_grad - row_dot)).astype(jnp.bfloat16)
        query_grad = (
            jnp.einsum("pqk,pkc->pqc", score_grad, key_heads, preferred_element_type=jnp.float32)
            * 0.125
        )
        key_grad = (
            key_grad
            + jnp.einsum(
                "pqk,pqc->pkc", score_grad, query_block, preferred_element_type=jnp.float32
            )
            * 0.125
        )
        value_grad = value_grad + jnp.einsum(
            "pqk,pqc->pkc",
            weights.astype(jnp.bfloat16),
            grad_block,
            preferred_element_type=jnp.float32,
        )
        return ((key_grad, value_grad), query_grad)

    empty = jnp.zeros((pair_count, length, head_size), jnp.float32)
    (key_grad, value_grad), query_grads = lax.scan(
        one_block, (empty, empty), (query_blocks, sum_blocks, grad_blocks)
    )
    query_grad = query_grads.transpose(1, 0, 2, 3).reshape(pair_count, length, head_size)
    return jnp.concatenate([query_grad, key_grad, value_grad], axis=-1)


def attention_forward(
    stream, norm_gain, norm_bias, qkv_weight, out_weight, out_bias, images, patches
):
    head_size = stream.shape[1] // HEADS
    normed = layer_norm(stream, norm_gain, norm_bias).astype(jnp.bfloat16)
    mixed = jnp.dot(normed, qkv_weight, preferred_element_type=jnp.float32).astype(jnp.bfloat16)
    arrived = lax.all_to_all(
        to_heads(mixed, images, patches, 3 * head_size),
        "blk",
        split_axis=0,
        concat_axis=1,
        tiled=True,
    )
    outputs, log_sums = local_attention(
        arrived[..., :head_size],
        arrived[..., head_size : 2 * head_size],
        arrived[..., 2 * head_size :],
    )
    returned = lax.all_to_all(
        outputs.astype(jnp.bfloat16), "blk", split_axis=1, concat_axis=0, tiled=True
    )
    attended = from_heads(returned, images, patches, head_size)
    branch = jnp.dot(attended, out_weight, preferred_element_type=jnp.float32) + out_bias
    return (stream + branch, (normed, arrived, log_sums, attended))


def attention_backward(
    stream_grad, stream, saved, norm_gain, norm_bias, qkv_weight, out_weight, images, patches
):
    normed, arrived, log_sums, attended = saved
    head_size = stream.shape[1] // HEADS
    branch_grad = stream_grad.astype(jnp.bfloat16)
    out_bias_grad = jnp.sum(branch_grad.astype(jnp.float32), axis=0)
    out_weight_grad = jnp.einsum(
        "ti,to->io", attended, branch_grad, preferred_element_type=jnp.float32
    )
    attended_grad = jnp.einsum(
        "to,io->ti", branch_grad, out_weight, preferred_element_type=jnp.float32
    ).astype(jnp.bfloat16)
    grad_heads = lax.all_to_all(
        to_heads(attended_grad, images, patches, head_size),
        "blk",
        split_axis=0,
        concat_axis=1,
        tiled=True,
    )
    mixed_grad = local_attention_back(
        arrived[..., :head_size],
        arrived[..., head_size : 2 * head_size],
        arrived[..., 2 * head_size :],
        log_sums,
        grad_heads,
    ).astype(jnp.bfloat16)
    returned = lax.all_to_all(mixed_grad, "blk", split_axis=1, concat_axis=0, tiled=True)
    mixed_flat = from_heads(returned, images, patches, 3 * head_size)
    qkv_weight_grad = jnp.einsum(
        "ti,to->io", normed, mixed_flat, preferred_element_type=jnp.float32
    )
    normed_grad = jnp.einsum(
        "to,io->ti", mixed_flat, qkv_weight, preferred_element_type=jnp.float32
    )
    unused, norm_back = jax.vjp(layer_norm, stream, norm_gain, norm_bias)
    input_grad, gain_grad, bias_grad = norm_back(normed_grad)
    return (
        stream_grad + input_grad,
        (gain_grad, bias_grad, qkv_weight_grad, out_weight_grad, out_bias_grad),
    )


def mlp_forward(stream, norm_gain, norm_bias, up_weight, up_bias, down_weight, down_bias):
    normed = layer_norm(stream, norm_gain, norm_bias).astype(jnp.bfloat16)
    hidden = jnp.dot(normed, up_weight, preferred_element_type=jnp.float32) + up_bias
    activated = gelu_exact(hidden).astype(jnp.bfloat16)
    branch = jnp.dot(activated, down_weight, preferred_element_type=jnp.float32) + down_bias
    return (stream + branch, (normed, hidden, activated))


def mlp_backward(stream_grad, stream, saved, norm_gain, norm_bias, up_weight, down_weight):
    normed, hidden, activated = saved
    branch_grad = stream_grad.astype(jnp.bfloat16)
    down_bias_grad = jnp.sum(branch_grad.astype(jnp.float32), axis=0)
    down_weight_grad = jnp.einsum(
        "tf,td->fd", activated, branch_grad, preferred_element_type=jnp.float32
    )
    act_grad = jnp.einsum("td,fd->tf", branch_grad, down_weight, preferred_element_type=jnp.float32)
    unused, gelu_back = jax.vjp(gelu_exact, hidden)
    hidden_grad = gelu_back(act_grad)[0].astype(jnp.bfloat16)
    up_bias_grad = jnp.sum(hidden_grad.astype(jnp.float32), axis=0)
    up_weight_grad = jnp.einsum(
        "td,tf->df", normed, hidden_grad, preferred_element_type=jnp.float32
    )
    normed_grad = jnp.einsum(
        "tf,df->td", hidden_grad, up_weight, preferred_element_type=jnp.float32
    )
    unused, norm_back = jax.vjp(layer_norm, stream, norm_gain, norm_bias)
    input_grad, gain_grad, bias_grad = norm_back(normed_grad)
    return (
        stream_grad + input_grad,
        (gain_grad, bias_grad, up_weight_grad, up_bias_grad, down_weight_grad, down_bias_grad),
    )


def owner_order(expert_major, blocks):
    local_experts, slot_rows, model_width = expert_major.shape
    capacity = slot_rows // blocks
    return (
        expert_major.reshape(local_experts, blocks, capacity, model_width)
        .transpose(1, 0, 2, 3)
        .reshape(blocks * local_experts, capacity, model_width)
    )


def expert_order(arrived, blocks, local_experts):
    total, capacity, model_width = arrived.shape
    return (
        arrived.reshape(blocks, local_experts, capacity, model_width)
        .transpose(1, 0, 2, 3)
        .reshape(local_experts, blocks * capacity, model_width)
    )


def per_device(
    tokens,
    attn_gain,
    attn_bias,
    w_qkv,
    w_out,
    b_out,
    mlp_gain,
    mlp_bias,
    w_up,
    b_up,
    w_down,
    b_down,
    moe_gain,
    moe_bias,
    router,
    expert_up,
    expert_up_bias,
    expert_down,
    expert_down_bias,
    priority,
    routes,
    out_grad,
):
    images, patches, model_width = tokens.shape
    tok_count = images * patches
    blocks = lax.axis_size("blk")
    experts = router.shape[1]
    local_experts = expert_up.shape[0]
    capacity = (21 * tok_count + 10 * experts - 1) // (10 * experts)
    slot_total = experts * capacity
    start = tokens.reshape(tok_count, model_width).astype(jnp.float32)
    first_out, first_saved = attention_forward(
        start, attn_gain[0], attn_bias[0], w_qkv[0], w_out[0], b_out[0], images, patches
    )
    middle, mlp_saved = mlp_forward(first_out, mlp_gain, mlp_bias, w_up, b_up, w_down, b_down)
    upper, second_saved = attention_forward(
        middle, attn_gain[1], attn_bias[1], w_qkv[1], w_out[1], b_out[1], images, patches
    )
    moe_normed = layer_norm(upper, moe_gain, moe_bias).astype(jnp.bfloat16)
    logits = jnp.dot(moe_normed, router, preferred_element_type=jnp.float32)
    gates = softmax_rows(logits)
    choices = routes.reshape(tok_count, 2)
    places, kept, kept_hits, dropped_hits = place_slots(
        priority.reshape(tok_count), choices, experts, capacity
    )
    labels = jnp.arange(experts, dtype=jnp.int32)
    picks = (choices[:, :, None] == labels[None, None, :]).astype(jnp.float32)
    gate_value = jnp.sum(picks * gates[:, None, :], axis=-1) * kept
    flat_places = places.reshape(2 * tok_count)
    targets = jnp.where(kept.reshape(2 * tok_count) > 0, flat_places, slot_total)
    sent_rows = jnp.broadcast_to(moe_normed[:, None, :], (tok_count, 2, model_width)).reshape(
        2 * tok_count, model_width
    )
    buffer = (
        jnp.zeros((slot_total, model_width), jnp.bfloat16).at[targets].set(sent_rows, mode="drop")
    )
    arrived = lax.all_to_all(
        buffer.reshape(experts, capacity, model_width),
        "blk",
        split_axis=0,
        concat_axis=0,
        tiled=True,
    )
    expert_rows = expert_order(arrived, blocks, local_experts)
    expert_hidden = (
        jnp.einsum("erd,edf->erf", expert_rows, expert_up, preferred_element_type=jnp.float32)
        + expert_up_bias[:, None, :]
    )
    expert_act = gelu_exact(expert_hidden).astype(jnp.bfloat16)
    expert_result = (
        jnp.einsum("erf,efd->erd", expert_act, expert_down, preferred_element_type=jnp.float32)
        + expert_down_bias[:, None, :]
    ).astype(jnp.bfloat16)
    returned = lax.all_to_all(
        owner_order(expert_result, blocks), "blk", split_axis=0, concat_axis=0, tiled=True
    )
    table = returned.reshape(slot_total, model_width)
    picked = table[flat_places].reshape(tok_count, 2, model_width).astype(jnp.float32)
    final = upper + jnp.sum(gate_value[:, :, None] * picked, axis=1)
    top_grad = out_grad.reshape(tok_count, model_width).astype(jnp.float32)
    gate_grad = jnp.sum(top_grad[:, None, :] * picked, axis=-1) * kept
    slot_rows_grad = (
        (gate_value[:, :, None] * top_grad[:, None, :])
        .astype(jnp.bfloat16)
        .reshape(2 * tok_count, model_width)
    )
    result_grad = (
        jnp.zeros((slot_total, model_width), jnp.bfloat16)
        .at[targets]
        .set(slot_rows_grad, mode="drop")
    )
    came_back = lax.all_to_all(
        result_grad.reshape(experts, capacity, model_width),
        "blk",
        split_axis=0,
        concat_axis=0,
        tiled=True,
    )
    out_rows_grad = expert_order(came_back, blocks, local_experts)
    down_bias_sum = jnp.sum(out_rows_grad.astype(jnp.float32), axis=1)
    down_sum = jnp.einsum(
        "erf,erd->efd", expert_act, out_rows_grad, preferred_element_type=jnp.float32
    )
    act_grad = jnp.einsum(
        "erd,efd->erf", out_rows_grad, expert_down, preferred_element_type=jnp.float32
    )
    unused, gelu_back = jax.vjp(gelu_exact, expert_hidden)
    hidden_grad = gelu_back(act_grad)[0].astype(jnp.bfloat16)
    up_bias_sum = jnp.sum(hidden_grad.astype(jnp.float32), axis=1)
    up_sum = jnp.einsum(
        "erd,erf->edf", expert_rows, hidden_grad, preferred_element_type=jnp.float32
    )
    rows_grad = jnp.einsum(
        "erf,edf->erd", hidden_grad, expert_up, preferred_element_type=jnp.float32
    ).astype(jnp.bfloat16)
    slot_grad = lax.all_to_all(
        owner_order(rows_grad, blocks), "blk", split_axis=0, concat_axis=0, tiled=True
    ).reshape(slot_total, model_width)
    normed_grad = jnp.sum(
        slot_grad[flat_places].reshape(tok_count, 2, model_width).astype(jnp.float32)
        * kept[:, :, None],
        axis=1,
    )
    gates_grad = jnp.sum(gate_grad[:, :, None] * picks, axis=1)
    unused, soft_back = jax.vjp(softmax_rows, logits)
    logit_grad = soft_back(gates_grad)[0].astype(jnp.bfloat16)
    router_sum = jnp.einsum("td,te->de", moe_normed, logit_grad, preferred_element_type=jnp.float32)
    normed_grad = normed_grad + jnp.einsum(
        "te,de->td", logit_grad, router, preferred_element_type=jnp.float32
    )
    unused, norm_back = jax.vjp(layer_norm, upper, moe_gain, moe_bias)
    upper_grad, moe_gain_sum, moe_bias_sum = norm_back(normed_grad)
    upper_grad = upper_grad + top_grad
    expert_sums = (
        lax.psum_scatter(up_sum.astype(jnp.bfloat16), "dp", scatter_dimension=1, tiled=True).astype(
            jnp.float32
        ),
        lax.psum_scatter(
            up_bias_sum.astype(jnp.bfloat16), "dp", scatter_dimension=1, tiled=True
        ).astype(jnp.float32),
        lax.psum_scatter(
            down_sum.astype(jnp.bfloat16), "dp", scatter_dimension=1, tiled=True
        ).astype(jnp.float32),
        lax.psum_scatter(
            down_bias_sum.astype(jnp.bfloat16), "dp", scatter_dimension=1, tiled=True
        ).astype(jnp.float32),
    )
    kept_float = kept_hits.astype(jnp.float32)
    dropped_float = dropped_hits.astype(jnp.float32)
    middle_grad, second_grads = attention_backward(
        upper_grad,
        middle,
        second_saved,
        attn_gain[1],
        attn_bias[1],
        w_qkv[1],
        w_out[1],
        images,
        patches,
    )
    second_gain, second_bias, second_qkv, second_proj, second_shift = second_grads
    first_out_grad, mlp_grads = mlp_backward(
        middle_grad, first_out, mlp_saved, mlp_gain, mlp_bias, w_up, w_down
    )
    mlp_gain_sum, mlp_bias_sum, up_weight_sum, up_bias_total, down_weight_sum, down_bias_total = (
        mlp_grads
    )
    start_grad, first_grads = attention_backward(
        first_out_grad,
        start,
        first_saved,
        attn_gain[0],
        attn_bias[0],
        w_qkv[0],
        w_out[0],
        images,
        patches,
    )
    first_gain, first_bias, first_qkv, first_proj, first_shift = first_grads
    everything = lax.psum(
        (
            first_gain,
            first_bias,
            first_qkv,
            first_proj,
            first_shift,
            second_gain,
            second_bias,
            second_qkv,
            second_proj,
            second_shift,
            mlp_gain_sum,
            mlp_bias_sum,
            up_weight_sum,
            up_bias_total,
            down_weight_sum,
            down_bias_total,
            moe_gain_sum,
            moe_bias_sum,
            router_sum,
            kept_float,
            dropped_float,
        ),
        ("dp", "blk"),
    )
    (
        first_gain,
        first_bias,
        first_qkv,
        first_proj,
        first_shift,
        second_gain,
        second_bias,
        second_qkv,
        second_proj,
        second_shift,
        mlp_gain_sum,
        mlp_bias_sum,
        up_weight_sum,
        up_bias_total,
        down_weight_sum,
        down_bias_total,
        moe_gain_sum,
        moe_bias_sum,
        router_sum,
        kept_float,
        dropped_float,
    ) = everything
    return (
        final.astype(jnp.bfloat16).reshape(images, patches, model_width),
        start_grad.reshape(images, patches, model_width),
        jnp.stack([first_gain, second_gain]),
        jnp.stack([first_bias, second_bias]),
        jnp.stack([first_qkv, second_qkv]),
        jnp.stack([first_proj, second_proj]),
        jnp.stack([first_shift, second_shift]),
        mlp_gain_sum,
        mlp_bias_sum,
        up_weight_sum,
        up_bias_total,
        down_weight_sum,
        down_bias_total,
        moe_gain_sum,
        moe_bias_sum,
        router_sum,
        expert_sums[0],
        expert_sums[1],
        expert_sums[2],
        expert_sums[3],
        kept_float.astype(jnp.int32),
        dropped_float.astype(jnp.int32),
    )


def solution(mesh):
    return jax.shard_map(
        per_device,
        mesh=mesh,
        in_specs=(
            P("dp", "blk", None),
            P(),
            P(),
            P(),
            P(),
            P(),
            P(),
            P(),
            P(),
            P(),
            P(),
            P(),
            P(),
            P(),
            P(),
            P("blk", None, None),
            P("blk", None),
            P("blk", None, None),
            P("blk", None),
            P(("dp", "blk"), None),
            P("dp", "blk", None),
            P("dp", "blk", None),
        ),
        out_specs=(
            P("dp", "blk", None),
            P("dp", "blk", None),
            P(),
            P(),
            P(),
            P(),
            P(),
            P(),
            P(),
            P(),
            P(),
            P(),
            P(),
            P(),
            P(),
            P(),
            P("blk", "dp", None),
            P("blk", "dp"),
            P("blk", "dp", None),
            P("blk", "dp"),
            P(),
            P(),
        ),
        check_vma=False,
    )
```

profile of v0, /device:TPU:0, one launch (start us, length us, event | category | flops | bytes accessed | tf_op | source)
XLA Modules:
  0.0 1077.1 jit_solution(17258394185384062895)
XLA Ops:
  15.0 3.5 convolution_convert_fusion.1
  21.1 3.5 reshape.730
  27.5 8.4 all-to-all-start
  35.9 34.2 %all-to-all-done = bf16[32,128,192]{1,2,0:T(8,128)(2,1)} async-done(((bf16[32,128,192]{1,2,0:T(8,128)(2,1)}), bf16[32,128,192]{1,2,0:T(8,128)(2,1)}, u32[]{:S(2)}, u32[]{:S(2)}) %all-to-all-start) | async-done | bytes 1572896 | tf_op jit(solution)/shard_map/all_to_all | solution.py:149
  73.8 28.0 %while.54 = (s32[]{:T(128)}, bf16[4,2,512,64]{2,3,1,0:T(8,128)(2,1)}, f32[4,2,512]{2,1,0:T(2,128)S(1)}, bf16[4,2,512,64]{2,3,1,0:T(8,128)(2,1)}, bf16[2,2048,64]...) while((s32[]{:T(128)}, bf16[4,2,512,64]{2,3,1,0:T(8,128)(2,1)}, ...), condition=%wide.region_5.6_spmd, body=%wide.region_2.5_spmd.sunk | while | flops 555744256 | bytes 30834840 | solution.py:89
  101.8 3.7 copy.237
  105.6 3.8 reshape.844
  109.4 7.9 all-to-all-start.1
  117.4 14.3 %all-to-all-done.1 = bf16[16,2,8192]{2,1,0:T(2,128)(2,1)} async-done(((bf16[16,2,8192]{2,1,0:T(2,128)(2,1)}), bf16[16,2,8192]{2,1,0:T(2,128)(2,1)}, u32[]{:S(2)}, u32[]{:S(2)}) %all-to-all-start.1) | async-done | bytes 524320 | tf_op jit(solution)/shard_map/all_to_all | solution.py:161
  131.6 3.7 reshape.845
  135.4 3.5 copy.239
  142.8 11.8 %multiply_convert_fusion.3 = (bf16[512,2048]{1,0:T(8,128)(2,1)S(1)}, f32[512,2048]{1,0:T(8,128)}, f32[512,2048]{1,0:T(8,128)}) fusion(f32[2048]{0:T(1024)S(1)} %copy-done.127, bf16[512,2048]{1,0:T(8,128)(2,1)S(1)} %copy-done.124, f32[512,512]{1,0:T(8,128)S(1)} %get-tuple-element.501, f32[512]{0:T(512)S(1)} %copy-done.88, f32[512]{0:T(512)S(1)} %copy-done.76, ...), kind=kOutput, calls=%fused_computation.114 | convolution fusion | flops 1144258560 | bytes 13647872 | tf_op jit(solution)/shard_map/dot_general | solution.py:214
  162.5 3.5 reshape.735
  168.9 4.4 all-to-all-start.2
  179.3 26.9 %all-to-all-done.2 = bf16[32,128,192]{1,2,0:T(8,128)(2,1)} async-done(((bf16[32,128,192]{1,2,0:T(8,128)(2,1)}), bf16[32,128,192]{1,2,0:T(8,128)(2,1)}, u32[]{:S(2)}, u32[]{:S(2)}) %all-to-all-start.2) | async-done | bytes 1572896 | tf_op jit(solution)/shard_map/all_to_all | solution.py:149
  210.0 28.0 %while.55 = (s32[]{:T(128)}, bf16[4,2,512,64]{2,3,1,0:T(8,128)(2,1)}, f32[4,2,512]{2,1,0:T(2,128)S(1)}, bf16[4,2,512,64]{2,3,1,0:T(8,128)(2,1)}, bf16[2,2048,64]...) while((s32[]{:T(128)}, bf16[4,2,512,64]{2,3,1,0:T(8,128)(2,1)}, ...), condition=%wide.region_13.14_spmd, body=%wide.region_10.13_spmd.sunk | while | flops 555744256 | bytes 30834840 | solution.py:89
  238.0 3.7 copy.240
  241.8 3.8 reshape.846
  245.6 7.8 all-to-all-start.3
  257.1 10.7 all-to-all-done.3
  267.8 3.7 reshape.847
  271.6 3.5 copy.242
  283.7 6.6 scatter_custom_fusion.1
  292.5 4.6 all-to-all-start.4
  300.2 3.6 mul.519
  305.9 7.2 scatter_custom_fusion.2
  315.2 7.5 all-to-all-done.4
  322.8 6.3 all-to-all-start.6
  331.3 23.8 %multiply_convert_fusion.2 = (bf16[1088,2048]{1,0:T(8,128)(2,1)}, f32[1088,2048]{1,0:T(8,128)}, f32[1088,2048]{1,0:T(8,128)}) fusion(f32[2048]{0:T(1024)S(1)} %bitcast.548, bf16[1088,512]{1,0:T(8,128)(2,1)} %reshape.746, bf16[1,512,2048]{2,1,0:T(8,128)(2,1)S(1)} %copy-done), kind=kOutput, calls=%fused_computation.95 | convolution fusion | flops 2428764160 | bytes 25501696 | tf_op jit(solution)/shard_map/erd,edf->erf/dot_general | solution.py:330
  357.3 11.2 %fusion.179 = (bf16[2048]{0:T(1024)(128)(2,1)}, bf16[1088,2048]{1,0:T(8,128)(2,1)S(1)}) fusion(f32[1088,2048]{1,0:T(8,128)} %get-tuple-element.467, f32[1088,2048]{1,0:T(8,128)} %get-tuple-element.507, bf16[1088,512]{1,0:T(8,128)(2,1)} %reshape.752, bf16[1,2048,512]{2,1,0:T(8,128)(2,1)} %param.47), kind=kOutput, calls=%fused_computation.348 | convolution fusion | flops 2315122688 | bytes 25497600 | tf_op jit(solution)/shard_map/erd,efd->erf/dot_general | solution.py:368
  370.5 3.5 convolution_convert_fusion.4
  376.2 7.0 all-to-all-start.7
  383.3 6.5 fusion.82
  392.0 17.0 %all-to-all-done.7 = bf16[16,68,512]{2,1,0:T(8,128)(2,1)S(1)} async-done(((bf16[16,68,512]{2,1,0:T(8,128)(2,1)}), bf16[16,68,512]{2,1,0:T(8,128)(2,1)S(1)}, u32[]{:S(2)}, u32[]{:S(2)}) %all-to-all-start.7) | async-done | bytes 1114144 | tf_op jit(solution)/shard_map/all_to_all | solution.py:380
  409.0 6.4 all-to-all-start.5
  419.2 5.1 gather_fusion.3
  424.3 16.9 %all-to-all-done.5 = bf16[16,68,512]{2,1,0:T(8,128)(2,1)} async-done(((bf16[16,68,512]{2,1,0:T(8,128)(2,1)}), bf16[16,68,512]{2,1,0:T(8,128)(2,1)}, u32[]{:S(2)}, u32[]{:S(2)}) %all-to-all-start.5) | async-done | bytes 1114144 | tf_op jit(solution)/shard_map/all_to_all | solution.py:338
  442.6 5.1 gather_fusion.2
  450.0 6.3 multiply_reduce_fusion.4
  458.1 3.4 reshape.770
  461.4 4.5 multiply_reduce_fusion.5
  472.7 7.0 all-to-all-start.8
  479.7 14.5 %all-to-all-done.8 = bf16[32,128,64]{1,2,0:T(8,128)(2,1)} async-done(((bf16[32,128,64]{1,2,0:T(8,128)(2,1)}), bf16[32,128,64]{1,2,0:T(8,128)(2,1)}, u32[]{:S(2)}, u32[]{:S(2)}) %all-to-all-start.8) | async-done | bytes 524320 | tf_op jit(solution)/shard_map/all_to_all | solution.py:182
  501.3 48.9 %while.56 = (s32[]{:T(128)}, f32[2,2048,64]{1,2,0:T(8,128)S(1)}, f32[2,2048,64]{1,2,0:T(8,128)S(1)}, bf16[4,2,512,64]{2,3,1,0:T(8,128)(2,1)}, bf16[4,2,512,64]{2...) while((s32[]{:T(128)}, f32[2,2048,64]{1,2,0:T(8,128)S(1)}, ...), condition=%wide.region_40.41_spmd.clone, body=%wide.region_38.40_spmd.clone.sunk | while | flops 1368718336 | bytes 75788520 | solution.py:136
  551.5 3.8 copy.223
  555.3 3.9 all-to-all-start.9
  563.0 6.8 fusion.84
  569.9 31.9 %all-to-all-done.9 = bf16[2,2048,192]{2,0,1:T(2,128)(2,1)S(1)} async-done(((bf16[2,2048,192]{2,0,1:T(2,128)(2,1)}), bf16[2,2048,192]{2,0,1:T(2,128)(2,1)S(1)}, u32[]{:S(2)}, u32[]{:S(2)}) %all-to-all-start.9) | async-done | bytes 1572896 | tf_op jit(solution)/shard_map/all_to_all | solution.py:196
  601.7 3.5 copy.244
  623.1 9.8 all-to-all-start.10
  633.2 6.9 fusion.83
  640.2 7.2 all-to-all-done.10
  654.4 51.5 %while.57 = (s32[]{:T(128)}, f32[2,2048,64]{1,2,0:T(8,128)S(1)}, f32[2,2048,64]{1,2,0:T(8,128)S(1)}, bf16[4,2,512,64]{2,3,1,0:T(8,128)(2,1)}, bf16[4,2,512,64]{2...) while((s32[]{:T(128)}, f32[2,2048,64]{1,2,0:T(8,128)S(1)}, ...), condition=%wide.region_47.48_spmd.clone, body=%wide.region_45.47_spmd.clone.sunk | while | flops 1368718336 | bytes 75788520 | solution.py:136
  707.3 3.8 copy.232
  711.1 4.6 all-to-all-start.11
  720.1 4.3 convolution_bitcast_fusion
  724.4 3.3 fusion.149
  727.8 3.5 fusion.158
  731.2 26.4 %all-to-all-done.11 = bf16[2,2048,192]{2,0,1:T(2,128)(2,1)} async-done(((bf16[2,2048,192]{2,0,1:T(2,128)(2,1)}), bf16[2,2048,192]{2,0,1:T(2,128)(2,1)}, u32[]{:S(2)}, u32[]{:S(2)}) %all-to-all-start.11) | async-done | bytes 1572896 | tf_op jit(solution)/shard_map/all_to_all | solution.py:196
  757.6 4.7 copy.246
  777.8 3.5 fusion.160
  782.9 48.4 %all-reduce = (f32[1,512]{1,0:T(1,128)S(1)}, f32[1,512]{1,0:T(1,128)S(1)}, f32[1,512]{1,0:T(1,128)S(1)}, f32[1,512]{1,0:T(1,128)S(1)}, f32[1,512]{1,0:T(1,128)S(...) all-reduce(f32[1,512]{1,0:T(1,128)S(1)} %bitcast.544, ...), channel_id=1, replica_groups=mesh['dp'=2,'blk'=16] {'dp','blk'}, use_global_device_ids=true, to_apply=%region_53.54 | all-reduce | flops 15904 | bytes 127232 | tf_op jit(solution)/shard_map/psum | solution.py:444
  836.2 218.5 %all-reduce.4.cloned.1.call-done = (f32[1,512,1536]{2,1,0:T(8,128)}, f32[1,512,1536]{2,1,0:T(8,128)}, f32[1,512,512]{2,1,0:T(8,128)}, f32[1,512,512]{2,1,0:T(8,1...) async-done(((f32[1,512,1536]{2,1,0:T(8,128)}, f32[1,512,1536]{2,1,0:T(8,128)}, f32[1,512,512]{2,1,0:T(8,128)}, f32[1,512,512]{2,1,0:T(8,128)}, f32[512,2048]{1,0:T(8,128)}, ...) | async-done | bytes 16777232 | tf_op jit(solution)/shard_map/psum | solution.py:444
  1054.7 6.1 pad_maximum_fusion
  (604 shorter events, 317.2 us)
Async XLA Ops:
  8.0 323.3 %copy-start = (bf16[1,512,2048]{2,1,0:T(8,128)(2,1)S(1)}, bf16[1,512,2048]{2,1,0:T(8,128)(2,1)}, u32[]{:S(2)}) copy-start(bf16[1,512,2048]{2,1,0:T(8,128)(2,1)} %param.45) | copy-start | bytes 6291460
  12.1 144.8 %copy-start.105 = (f32[1,512]{1,0:T(1,128)}, f32[1,512]{1,0:T(1,128)S(1)}, u32[]{:S(2)}) copy-start(f32[1,512]{1,0:T(1,128)S(1)} %get-tuple-element.488) | copy-start | bytes 6148
  12.9 144.1 %copy-start.110 = (f32[1,512]{1,0:T(1,128)}, f32[1,512]{1,0:T(1,128)S(1)}, u32[]{:S(2)}) copy-start(f32[1,512]{1,0:T(1,128)S(1)} %get-tuple-element.490) | copy-start | bytes 6148
  27.5 42.6 %all-to-all-start = ((bf16[32,128,192]{1,2,0:T(8,128)(2,1)}), bf16[32,128,192]{1,2,0:T(8,128)(2,1)}, u32[]{:S(2)}, u32[]{:S(2)}) async-start(bf16[32,128,192]{1,2,0:T(8,128)(2,1)} %bitcast.479), calls=%async_computation | async-start | bytes 3145728 | tf_op jit(solution)/shard_map/all_to_all | solution.py:149
  101.8 38.6 %copy-start.2 = (bf16[2,2048,64]{1,2,0:T(8,128)(2,1)}, bf16[2,2048,64]{1,2,0:T(8,128)(2,1)S(1)}, u32[]{:S(2)}) copy-start(bf16[2,2048,64]{1,2,0:T(8,128)(2,1)S(1)} %get-tuple-element.866) | copy-start | bytes 1572868
  101.8 38.6 %copy-start.6 = (bf16[2,2048,64]{1,2,0:T(8,128)(2,1)}, bf16[2,2048,64]{1,2,0:T(8,128)(2,1)S(1)}, u32[]{:S(2)}) copy-start(bf16[2,2048,64]{1,2,0:T(8,128)(2,1)S(1)} %get-tuple-element.870) | copy-start | bytes 1572868
  101.8 38.6 %copy-start.66 = (f32[4,2,512]{2,1,0:T(2,128)}, f32[4,2,512]{2,1,0:T(2,128)S(1)}, u32[]{:S(2)}) copy-start(f32[4,2,512]{2,1,0:T(2,128)S(1)} %get-tuple-element.801) | copy-start | bytes 49156
  101.8 15.5 %copy-start.117 = (f32[2,512]{1,0:T(2,128)S(1)}, f32[2,512]{1,0:T(2,128)}, u32[]{:S(2)}) copy-start(f32[2,512]{1,0:T(2,128)} %param.35) | copy-start | bytes 12292
  109.4 22.3 %all-to-all-start.1 = ((bf16[16,2,8192]{2,1,0:T(2,128)(2,1)}), bf16[16,2,8192]{2,1,0:T(2,128)(2,1)}, u32[]{:S(2)}, u32[]{:S(2)}) async-start(bf16[16,2,8192]{2,1,0:T(2,128)(2,1)} %reshape.844), calls=%async_computation.1 | async-start | bytes 1048576 | tf_op jit(solution)/shard_map/all_to_all | solution.py:161
  117.3 25.4 %copy-start.76 = (f32[512]{0:T(512)S(1)}, f32[512]{0:T(512)}, u32[]{:S(2)}) copy-start(f32[512]{0:T(512)} %param.36) | copy-start | bytes 6148
  117.3 25.4 %copy-start.88 = (f32[512]{0:T(512)S(1)}, f32[512]{0:T(512)}, u32[]{:S(2)}) copy-start(f32[512]{0:T(512)} %param.37) | copy-start | bytes 6148
  117.3 25.4 %copy-start.127 = (f32[2048]{0:T(1024)S(1)}, f32[2048]{0:T(1024)}, u32[]{:S(2)}) copy-start(f32[2048]{0:T(1024)} %param.39) | copy-start | bytes 24580
  142.4 12.2 %copy-start.18 = (f32[512,512]{1,0:T(8,128)}, f32[512,512]{1,0:T(8,128)S(1)}, u32[]{:S(2)}) copy-start(f32[512,512]{1,0:T(8,128)S(1)} %get-tuple-element.501) | copy-start | bytes 3145732
  142.5 12.2 %copy-start.72 = (f32[512]{0:T(512)}, f32[512]{0:T(512)S(1)}, u32[]{:S(2)}) copy-start(f32[512]{0:T(512)S(1)} %broadcast_multiply_fusion.3) | copy-start | bytes 6148
  142.7 11.9 %copy-start.91 = (f32[512]{0:T(512)}, f32[512]{0:T(512)S(1)}, u32[]{:S(2)}) copy-start(f32[512]{0:T(512)S(1)} %multiply_reduce_fusion.17) | copy-start | bytes 6148
  142.8 11.8 %copy-start.82 = (f32[512]{0:T(512)}, f32[512]{0:T(512)S(1)}, u32[]{:S(2)}) copy-start(f32[512]{0:T(512)S(1)} %fusion.143) | copy-start | bytes 6148
  142.8 11.8 %copy-start.122 = (bf16[2048,512]{1,0:T(8,128)(2,1)S(1)}, bf16[2048,512]{1,0:T(8,128)(2,1)}, u32[]{:S(2)}) copy-start(bf16[2048,512]{1,0:T(8,128)(2,1)} %param.40) | copy-start | bytes 6291460
  142.8 11.8 %copy-start.129 = (f32[512]{0:T(512)S(1)}, f32[512]{0:T(512)}, u32[]{:S(2)}) copy-start(f32[512]{0:T(512)} %param.41) | copy-start | bytes 6148
  162.5 10.9 %copy-start.107 = (s32[4,128,2]{1,2,0:T(2,128)S(1)}, s32[4,128,2]{1,2,0:T(2,128)}, u32[]{:S(2)}) copy-start(s32[4,128,2]{1,2,0:T(2,128)} %param.50) | copy-start | bytes 12292
  168.9 37.4 %all-to-all-start.2 = ((bf16[32,128,192]{1,2,0:T(8,128)(2,1)}), bf16[32,128,192]{1,2,0:T(8,128)(2,1)}, u32[]{:S(2)}, u32[]{:S(2)}) async-start(bf16[32,128,192]{1,2,0:T(8,128)(2,1)} %bitcast.478), calls=%async_computation.2 | async-start | bytes 3145728 | tf_op jit(solution)/shard_map/all_to_all | solution.py:149
  179.3 30.6 %copy-start.109 = (s32[16,5]{0,1:T(8,128)}, s32[16,5]{0,1:T(8,128)S(1)}, u32[]{:S(2)}) copy-start(s32[16,5]{0,1:T(8,128)S(1)} %reduce-window.19) | copy-start | bytes 964
  238.0 17.1 %copy-start.8 = (bf16[2,2048,64]{1,2,0:T(8,128)(2,1)}, bf16[2,2048,64]{1,2,0:T(8,128)(2,1)S(1)}, u32[]{:S(2)}) copy-start(bf16[2,2048,64]{1,2,0:T(8,128)(2,1)S(1)} %get-tuple-element.871) | copy-start | bytes 1572868
  238.0 17.0 %slice-start = ((s32[16,5]{0,1:T(8,128)}), s32[16,4]{0,1:T(4,128)S(1)}, s32[]{:S(2)}) async-start(s32[16,5]{0,1:T(8,128)} %copy-done.109), calls=%async_computation.21 | async-start | bytes 4096 | tf_op jit(solution)/shard_map/slice.3
  245.6 22.3 %all-to-all-start.3 = ((bf16[16,2,8192]{2,1,0:T(2,128)(2,1)}), bf16[16,2,8192]{2,1,0:T(2,128)(2,1)}, u32[]{:S(2)}, u32[]{:S(2)}) async-start(bf16[16,2,8192]{2,1,0:T(2,128)(2,1)} %reshape.846), calls=%async_computation.3 | async-start | bytes 1048576 | tf_op jit(solution)/shard_map/all_to_all | solution.py:161
  256.3 22.6 %copy-start.40 = (s32[512,2]{1,0:T(8,128)}, s32[512,2]{1,0:T(8,128)S(1)}, u32[]{:S(2)}) copy-start(s32[512,2]{1,0:T(8,128)S(1)} %gather_fusion.1) | copy-start | bytes 12292
  257.1 26.6 %copy-start.118 = (s32[1024,1]{0,1:T(1,128)}, s32[1024,1]{0,1:T(1,128)S(1)}, u32[]{:S(2)}) copy-start(s32[1024,1]{0,1:T(1,128)S(1)} %get-tuple-element.487) | copy-start | bytes 12292
  257.1 22.6 %copy-start.99 = (f32[512]{0:T(512)S(1)}, f32[512]{0:T(512)}, u32[]{:S(2)}) copy-start(f32[512]{0:T(512)} %param.42) | copy-start | bytes 6148
  257.1 22.6 %copy-start.119 = (f32[512]{0:T(512)S(1)}, f32[512]{0:T(512)}, u32[]{:S(2)}) copy-start(f32[512]{0:T(512)} %param.43) | copy-start | bytes 6148
  278.7 13.8 %copy-start.74 = (f32[512]{0:T(512)}, f32[512]{0:T(512)S(1)}, u32[]{:S(2)}) copy-start(f32[512]{0:T(512)S(1)} %broadcast_multiply_fusion.1) | copy-start | bytes 6148
  278.9 13.6 %copy-start.95 = (f32[512]{0:T(512)}, f32[512]{0:T(512)S(1)}, u32[]{:S(2)}) copy-start(f32[512]{0:T(512)S(1)} %multiply_reduce_fusion.15) | copy-start | bytes 6148
  279.7 12.8 %copy-start.86 = (f32[512]{0:T(512)}, f32[512]{0:T(512)S(1)}, u32[]{:S(2)}) copy-start(f32[512]{0:T(512)S(1)} %fusion.145) | copy-start | bytes 6148
  280.0 24.6 %copy-start.23 = (bf16[512,512]{1,0:T(8,128)(2,1)}, bf16[512,512]{1,0:T(8,128)(2,1)S(1)}, u32[]{:S(2)}) copy-start(bf16[512,512]{1,0:T(8,128)(2,1)S(1)} %add_convert_fusion.3) | copy-start | bytes 1572868
  292.5 30.3 %all-to-all-start.4 = ((bf16[16,68,512]{2,1,0:T(8,128)(2,1)}), bf16[16,68,512]{2,1,0:T(8,128)(2,1)}, u32[]{:S(2)}, u32[]{:S(2)}) async-start(bf16[16,68,512]{2,1,0:T(8,128)(2,1)} %reshape.745), calls=%async_computation.4 | async-start | bytes 2359296 | tf_op jit(solution)/shard_map/all_to_all | solution.py:321
  297.2 159.2 %copy-start.70 = (s32[512,2]{0,1:T(2,128)}, s32[512,2]{0,1:T(2,128)S(1)}, u32[]{:S(2)}) copy-start(s32[512,2]{0,1:T(2,128)S(1)} %copy.214) | copy-start | bytes 12292
  305.5 160.4 %copy-start.67 = (pred[512,16]{0,1:T(8,128)(4,1)}, pred[512,16]{0,1:T(8,128)(4,1)S(1)}, u32[]{:S(2)}) copy-start(pred[512,16]{0,1:T(8,128)(4,1)S(1)} %get-tuple-element.465) | copy-start | bytes 24580
  313.1 18.2 %copy-start.126 = (f32[1,2048]{1,0:T(1,128)S(1)}, f32[1,2048]{1,0:T(1,128)}, u32[]{:S(2)}) copy-start(f32[1,2048]{1,0:T(1,128)} %param.46) | copy-start | bytes 24580
  322.8 32.3 %all-to-all-start.6 = ((bf16[16,68,512]{2,1,0:T(8,128)(2,1)}), bf16[16,68,512]{2,1,0:T(8,128)(2,1)}, u32[]{:S(2)}, u32[]{:S(2)}) async-start(bf16[16,68,512]{2,1,0:T(8,128)(2,1)} %reshape.751), calls=%async_computation.6 | async-start | bytes 2359296 | tf_op jit(solution)/shard_map/all_to_all | solution.py:356
  376.2 32.8 %all-to-all-start.7 = ((bf16[16,68,512]{2,1,0:T(8,128)(2,1)}), bf16[16,68,512]{2,1,0:T(8,128)(2,1)S(1)}, u32[]{:S(2)}, u32[]{:S(2)}) async-start(bf16[16,68,512]{2,1,0:T(8,128)(2,1)} %reshape_transpose_reshape.9), calls=%async_computation.7 | async-start | bytes 2359296 | tf_op jit(solution)/shard_map/all_to_all | solution.py:380
  389.7 26.4 %copy-start.25 = (bf16[4,128,512]{2,1,0:T(8,128)(2,1)S(1)}, bf16[4,128,512]{2,1,0:T(8,128)(2,1)}, u32[]{:S(2)}) copy-start(bf16[4,128,512]{2,1,0:T(8,128)(2,1)} %param.51) | copy-start | bytes 1572868
  389.7 27.5 %copy-start.108 = (s32[1024,1]{0,1:T(1,128)S(1)}, s32[1024,1]{0,1:T(1,128)}, u32[]{:S(2)}) copy-start(s32[1024,1]{0,1:T(1,128)} %get-tuple-element.486) | copy-start | bytes 12292
  389.7 27.5 %copy-start.81 = (f32[512]{0:T(512)S(1)}, f32[512]{0:T(512)}, u32[]{:S(2)}) copy-start(f32[512]{0:T(512)} %copy-done.80) | copy-start | bytes 6148
  409.0 32.2 %all-to-all-start.5 = ((bf16[16,68,512]{2,1,0:T(8,128)(2,1)}), bf16[16,68,512]{2,1,0:T(8,128)(2,1)}, u32[]{:S(2)}, u32[]{:S(2)}) async-start(bf16[16,68,512]{2,1,0:T(8,128)(2,1)} %reshape_transpose_reshape.8), calls=%async_computation.5 | async-start | bytes 2359296 | tf_op jit(solution)/shard_map/all_to_all | solution.py:338
  469.2 10.5 copy-start.21
  471.4 29.9 %copy-start.9 = (bf16[2,2048,64]{1,2,0:T(8,128)(2,1)S(1)}, bf16[2,2048,64]{1,2,0:T(8,128)(2,1)}, u32[]{:S(2)}) copy-start(bf16[2,2048,64]{1,2,0:T(8,128)(2,1)} %copy-done.8) | copy-start | bytes 1572868
  472.7 21.6 %all-to-all-start.8 = ((bf16[32,128,64]{1,2,0:T(8,128)(2,1)}), bf16[32,128,64]{1,2,0:T(8,128)(2,1)}, u32[]{:S(2)}, u32[]{:S(2)}) async-start(bf16[32,128,64]{1,2,0:T(8,128)(2,1)} %bitcast.58), calls=%async_computation.8 | async-start | bytes 1048576 | tf_op jit(solution)/shard_map/all_to_all | solution.py:182
  555.3 46.4 %all-to-all-start.9 = ((bf16[2,2048,192]{2,0,1:T(2,128)(2,1)}), bf16[2,2048,192]{2,0,1:T(2,128)(2,1)S(1)}, u32[]{:S(2)}, u32[]{:S(2)}) async-start(bf16[2,2048,192]{2,0,1:T(2,128)(2,1)} %copy.223), calls=%async_computation.9 | async-start | bytes 4194304 | tf_op jit(solution)/shard_map/all_to_all | solution.py:196
  559.2 209.4 %reduce-scatter.15.cloned.1.call-start = ((), (), s32[]{:S(2)}) async-start(), calls=%async_computation.19 | async-start | bytes 196608
  561.6 208.6 %reduce-scatter.13.cloned.1.call-start = ((), (), s32[]{:S(2)}) async-start(), calls=%async_computation.18 | async-start | bytes 786432
  562.8 209.2 %reduce-scatter.11.cloned.1.call-start = ((), (), s32[]{:S(2)}) async-start(), calls=%async_computation.17 | async-start | bytes 3145728 | tf_op jit(solution)/shard_map/reduce_scatter | solution.py:405
  569.8 38.1 %copy-start.13 = (f32[512,512]{1,0:T(8,128)S(1)}, f32[512,512]{1,0:T(8,128)}, u32[]{:S(2)}) copy-start(f32[512,512]{1,0:T(8,128)} %copy-done.12) | copy-start | bytes 3145732
  569.8 38.1 %copy-start.85 = (f32[512]{0:T(512)S(1)}, f32[512]{0:T(512)}, u32[]{:S(2)}) copy-start(f32[512]{0:T(512)} %copy-done.84) | copy-start | bytes 6148
  569.8 38.1 %copy-start.104 = (f32[512]{0:T(512)S(1)}, f32[512]{0:T(512)}, u32[]{:S(2)}) copy-start(f32[512]{0:T(512)} %copy-done.103) | copy-start | bytes 6148
  569.8 38.1 %copy-start.106 = (f32[1,512]{1,0:T(1,128)S(1)}, f32[1,512]{1,0:T(1,128)}, u32[]{:S(2)}) copy-start(f32[1,512]{1,0:T(1,128)} %copy-done.105) | copy-start | bytes 6148
  623.1 24.3 %all-to-all-start.10 = ((bf16[32,128,64]{1,2,0:T(8,128)(2,1)}), bf16[32,128,64]{1,2,0:T(8,128)(2,1)}, u32[]{:S(2)}, u32[]{:S(2)}) async-start(bf16[32,128,64]{1,2,0:T(8,128)(2,1)} %bitcast.69), calls=%async_computation.10 | async-start | bytes 1048576 | tf_op jit(solution)/shard_map/all_to_all | solution.py:182
  633.0 141.9 %reduce-scatter.9.cloned.1.call-start = ((), (), s32[]{:S(2)}) async-start(), calls=%async_computation.16 | async-start | bytes 3145728 | tf_op jit(solution)/shard_map/reduce_scatter | solution.py:399
  640.1 14.3 %copy-start.3 = (bf16[2,2048,64]{1,2,0:T(8,128)(2,1)S(1)}, bf16[2,2048,64]{1,2,0:T(8,128)(2,1)}, u32[]{:S(2)}) copy-start(bf16[2,2048,64]{1,2,0:T(8,128)(2,1)} %copy-done.2) | copy-start | bytes 1572868
  640.1 14.3 %copy-start.7 = (bf16[2,2048,64]{1,2,0:T(8,128)(2,1)S(1)}, bf16[2,2048,64]{1,2,0:T(8,128)(2,1)}, u32[]{:S(2)}) copy-start(bf16[2,2048,64]{1,2,0:T(8,128)(2,1)} %copy-done.6) | copy-start | bytes 1572868
  711.1 46.5 %all-to-all-start.11 = ((bf16[2,2048,192]{2,0,1:T(2,128)(2,1)}), bf16[2,2048,192]{2,0,1:T(2,128)(2,1)}, u32[]{:S(2)}, u32[]{:S(2)}) async-start(bf16[2,2048,192]{2,0,1:T(2,128)(2,1)} %copy.232), calls=%async_computation.11 | async-start | bytes 4194304 | tf_op jit(solution)/shard_map/all_to_all | solution.py:196
  715.7 339.0 %all-reduce.4.cloned.1.call-start = ((), (), s32[]{:S(2)}) async-start(), calls=%async_computation.20 | async-start | bytes 33554432 | tf_op jit(solution)/shard_map/psum | solution.py:444
  731.2 33.5 %copy-start.43 = (bf16[4,128,512]{2,1,0:T(8,128)(2,1)S(1)}, bf16[4,128,512]{2,1,0:T(8,128)(2,1)}, u32[]{:S(2)}) copy-start(bf16[4,128,512]{2,1,0:T(8,128)(2,1)} %copy-done.42) | copy-start | bytes 1572868
  767.5 10.3 copy-start.15
  767.5 10.3 copy-start.79
  767.5 10.3 copy-start.90
  777.8 55.7 %copy-start.17 = (f32[512,512]{1,0:T(8,128)S(1)}, f32[512,512]{1,0:T(8,128)}, u32[]{:S(2)}) copy-start(f32[512,512]{1,0:T(8,128)} %copy-done.16) | copy-start | bytes 3145732
  (118 other events, 411.6 us)
Sparse Core Ops, SparseCore 0:
  562.3 8.7 reduce-scatter.14
  573.5 9.1 reduce-scatter.12
  584.9 10.7 reduce-scatter.10
  640.3 10.8 reduce-scatter.8
Sparse Core Ops, SparseCore 1:
  767.5 287.1 all-reduce.3
where the time goes:
time: 1090 us; the launch traced here: 1080 us
  waiting for transfers between devices  426 us (39%)
  matrix products  231 us (21%)
  local copies, waits for them, and re-layouts  187 us (17%)
  other arithmetic  87.8 us (8%)
  starting transfers between devices  79 us (7%)
  blocking collectives  48.4 us (4%)
  between operations  17.4 us (2%)
    psum x1, waiting for transfers between devices, per_device(): lax.psum((first_gain, first_bias, first_qkv, first_proj, first_shift, sec...  219 us
    all_to_all x2, waiting for transfers between devices, attention_forward(): lax.all_to_all(to_heads(mixed, images, patches, 3 * head_size), 'blk', sp...  61.2 us
    all_to_all x2, waiting for transfers between devices, attention_backward(): lax.all_to_all(mixed_grad, 'blk', split_axis=1, concat_axis=0, tiled=True)  58.2 us
    psum x1, blocking collectives, per_device(): lax.psum((first_gain, first_bias, first_qkv, first_proj, first_shift, sec...  48.4 us
    unnamed x261, local copies, waits for them, and re-layouts  43.2 us
    dot_general x16, matrix products, one_block(): jnp.einsum('pqc,pkc->pqk', query_block, key_heads, preferred_element_type...  36.2 us
    all_to_all x2, waiting for transfers between devices, attention_forward(): lax.all_to_all(outputs.astype(jnp.bfloat16), 'blk', split_axis=1, concat_...  25 us
    dot_general x1, matrix products, per_device(): jnp.einsum('erd,edf->erf', expert_rows, expert_up, preferred_element_type...  23.8 us
  transfers between devices with their start and end apart: 17, of which 12 were waited for; matrix products, arithmetic and copies ran while one was open for 20% of the time, Pallas kernels for 0%

commit v1 on v0

v1 whole, which is shorter than its diff:
```python
import math

import jax
import jax.numpy as jnp
from jax import lax
from jax.experimental import pallas as pl
from jax.experimental.pallas import tpu as pltpu
from jax.sharding import PartitionSpec as P

HEADS = 8

epsilon = 1e-06
log2_e = 1.4426950408889634
MIB = 1024 * 1024


def split3(values):
    high = values.astype(jnp.bfloat16)
    rest = values - high.astype(jnp.float32)
    middle = rest.astype(jnp.bfloat16)
    low = (rest - middle.astype(jnp.float32)).astype(jnp.bfloat16)
    return (high, middle, low)


def abt(left, right):
    return lax.dot_general(
        left, right, (((1,), (1,)), ((), ())), preferred_element_type=jnp.float32
    )


def ab(left, right):
    return jnp.dot(left, right, preferred_element_type=jnp.float32)


def atb(left, right):
    return lax.dot_general(
        left, right, (((0,), (0,)), ((), ())), preferred_element_type=jnp.float32
    )


def normalize(stream):
    centre = jnp.mean(stream, axis=1, keepdims=True)
    shifted = stream - centre
    spread = jnp.mean(shifted * shifted, axis=1, keepdims=True)
    scale = lax.rsqrt(spread + epsilon)
    return (shifted * scale, scale)


def norm_back(stream, norm_gain, normed_grad):
    hat, scale = normalize(stream)
    gain_grad = jnp.sum(normed_grad * hat, axis=0, keepdims=True)
    bias_grad = jnp.sum(normed_grad, axis=0, keepdims=True)
    inner = normed_grad * norm_gain
    along = jnp.mean(inner * hat, axis=1, keepdims=True)
    level = jnp.mean(inner, axis=1, keepdims=True)
    return (scale * (inner - level - hat * along), gain_grad, bias_grad)


def gelu_parts(values):
    size = jnp.abs(values)
    bell = jnp.exp2(values * values * (-0.5 * log2_e))
    t = 1.0 / (1.0 + size * (0.3275911 * math.sqrt(0.5)))
    series = t * (
        0.127414796
        + t * (-0.142248368 + t * (0.7107068705 + t * (-0.7265760135 + t * 0.5307027145)))
    )
    tail = series * bell
    cdf = jnp.where(values < 0, tail, 1.0 - tail)
    return (values * cdf, cdf + values * bell * (1.0 / math.sqrt(2.0 * math.pi)))


def call(kernel, name, operands, outs, flops, grid=(1,), specs=None, out_specs=None, scratch=(), limit=60):
    whole = lambda shape: pl.BlockSpec(shape, lambda *steps: (0,) * len(shape))
    specs = dict(specs or {})
    out_specs = out_specs or {}
    for number, operand in enumerate(operands):
        if operand.dtype == jnp.int32 and operand.shape == (1,):
            specs[number] = pl.BlockSpec(memory_space=pltpu.SMEM)
    return pl.pallas_call(
        kernel,
        grid=grid,
        in_specs=[specs.get(i, whole(array.shape)) for i, array in enumerate(operands)],
        out_specs=[out_specs.get(i, whole(out.shape)) for i, out in enumerate(outs)],
        out_shape=outs,
        scratch_shapes=list(scratch),
        compiler_params=pltpu.CompilerParams(vmem_limit_bytes=limit * MIB),
        cost_estimate=pl.CostEstimate(
            flops=flops,
            bytes_accessed=sum(a.size * a.dtype.itemsize for a in operands)
            + sum(o.size * o.dtype.itemsize for o in outs),
            transcendentals=0,
        ),
        name=name,
    )(*operands)


def layer_spec(array, layer):
    return pl.BlockSpec((None,) + array.shape[1:], lambda *steps: (layer, 0, 0))


def bf16(*shape):
    return jax.ShapeDtypeStruct(shape, jnp.bfloat16)


def f32(*shape):
    return jax.ShapeDtypeStruct(shape, jnp.float32)


def ahead(place, shift, count):
    return lax.rem(place + shift, count)


def block_at(number, size):
    return pl.ds(pl.multiple_of(number * size, size), size)


def attention_block(length):
    return min(length, 2**21 // length)


def attention(mixed, head_size, local_heads, order):
    length = mixed.shape[0]
    block = attention_block(length)
    scale = head_size**-0.5

    def kernel(mixed_ref, out_ref, plain_ref, query_ref, keys, values):
        step = pl.program_id(0)

        @pl.when(step == 0)
        def _():
            for head in range(local_heads):
                base = head * 3 * head_size
                key = mixed_ref[:, base + head_size : base + 2 * head_size]
                value = mixed_ref[:, base + 2 * head_size : base + 3 * head_size]
                keys[head] = jnp.concatenate([key, key], axis=1)
                values[head] = jnp.concatenate(
                    [value, jnp.ones((length, head_size), jnp.bfloat16)], axis=1
                )

        rows = pl.ds(pl.multiple_of(step * block, block), block)
        scores = []
        for head in range(local_heads):
            base = head * 3 * head_size
            query = mixed_ref[rows, base : base + head_size].astype(jnp.float32) * (scale * log2_e)
            high = query.astype(jnp.bfloat16)
            low = (query - high.astype(jnp.float32)).astype(jnp.bfloat16)
            pair = jnp.concatenate([high, low], axis=1)
            query_ref[:, head * 4 * head_size : head * 4 * head_size + 2 * head_size] = pair
            scores.append(abt(pair, keys[head]))
        outs = []
        for head in range(local_heads):
            largest = jnp.max(scores[head], axis=1, keepdims=True)
            weights = jnp.exp2(scores[head] - largest).astype(jnp.bfloat16)
            total = ab(weights, values[head])
            sums = total[:, head_size : head_size + 1]
            outs.append(total[:, :head_size] / sums)
            log_sum = largest + jnp.log2(sums)
            lane = lax.broadcasted_iota(jnp.int32, (block, 2 * head_size), 1)
            extra = jnp.zeros((block, 2 * head_size), jnp.float32)
            for place, digit in enumerate(split3(log_sum)):
                extra = jnp.where(lane == place, digit.astype(jnp.float32), extra)
            query_ref[:, head * 4 * head_size + 2 * head_size : (head + 1) * 4 * head_size] = (
                extra.astype(jnp.bfloat16)
            )
        both = jnp.concatenate(outs, axis=1)
        plain_ref[...] = both
        both = both.astype(jnp.bfloat16)
        if order is None:
            out_ref[rows, :] = both
        else:
            images, per = order
            size = length // (images * per)
            count = block // size
            for piece in range(count):
                number = step * count + piece
                place = lax.rem(number, images) * per + lax.div(number, images)
                target = pl.ds(pl.multiple_of(place * size, size), size)
                out_ref[target, :] = both[piece * size : (piece + 1) * size]

    return call(
        kernel,
        "attention",
        [mixed],
        [
            bf16(length, local_heads * head_size),
            f32(length, local_heads * head_size),
            bf16(length, local_heads * 4 * head_size),
        ],
        local_heads * length * length * 16 * head_size,
        grid=(length // block,),
        out_specs={
            1: pl.BlockSpec((block, local_heads * head_size), lambda step: (step, 0)),
            2: pl.BlockSpec((block, local_heads * 4 * head_size), lambda step: (step, 0)),
        },
        scratch=[
            pltpu.VMEM((local_heads, length, 2 * head_size), jnp.bfloat16),
            pltpu.VMEM((local_heads, length, 2 * head_size), jnp.bfloat16),
        ],
    )


def attention_back(mixed, queries, outs, grads, head_size, local_heads, order, flops):
    length = mixed.shape[0]
    block = attention_block(length)
    chunk = length // 4
    scale = head_size**-0.5

    def kernel(
        mixed_hbm, query_hbm, out_hbm, grad_hbm, mixed_grad_ref, grads, query_grads, weights,
        score_grads, mixed_ref, query_ref, out_ref, grad_ref, semaphores,
    ):
        step = pl.program_id(0)

        @pl.when(step == 0)
        def _():
            copies = [
                pltpu.make_async_copy(source, target, semaphores.at[place])
                for place, (source, target) in enumerate(
                    [
                        (grad_hbm, grad_ref), (out_hbm, out_ref), (mixed_hbm, mixed_ref),
                        (query_hbm, query_ref),
                    ]
                )
            ]
            for copy in copies:
                copy.start()
            copies[0].wait()
            copies[1].wait()
            query_grads[...] = jnp.zeros_like(query_grads)
            pieces = [(0, 0, length)]
            if order is not None:
                images, per = order
                size = length // (images * per)
                pieces = [
                    ((row * per + column) * size, (column * images + row) * size, size)
                    for row in range(images)
                    for column in range(per)
                ]
            for source, target, size in pieces:
                for head in range(local_heads):
                    columns = slice(head * head_size, (head + 1) * head_size)
                    grad = grad_ref[source : source + size, columns]
                    out = out_ref[target : target + size, columns]
                    dots = jnp.sum(grad.astype(jnp.float32) * out, axis=1, keepdims=True)
                    lane = lax.broadcasted_iota(jnp.int32, (size, head_size), 1)
                    extra = jnp.zeros((size, head_size), jnp.float32)
                    for place, digit in enumerate(split3(dots)):
                        extra = jnp.where(lane == place, digit.astype(jnp.float32), extra)
                    grads[head, target : target + size, :] = jnp.concatenate(
                        [grad, extra.astype(jnp.bfloat16)], axis=1
                    )
            copies[2].wait()
            copies[3].wait()

        rows = pl.ds(pl.multiple_of(step * block, block), block)
        for head in range(local_heads):
            base = head * 3 * head_size
            key = mixed_ref[rows, base + head_size : base + 2 * head_size]
            value = mixed_ref[rows, base + 2 * head_size : base + 3 * head_size]
            lane = lax.broadcasted_iota(jnp.int32, (block, 2 * head_size), 1)
            minus = jnp.where(lane < 3, -1.0, 0.0).astype(jnp.bfloat16)
            keys = jnp.concatenate([key, key, minus], axis=1)
            values = jnp.concatenate([value, minus[:, :head_size]], axis=1)
            for piece in range(length // chunk):
                span = slice(piece * chunk, (piece + 1) * chunk)
                scores = abt(keys, query_ref[span, head * 4 * head_size : (head + 1) * 4 * head_size])
                weight = jnp.exp2(scores)
                weights[head, :, span] = weight.astype(jnp.bfloat16)
                score_grads[head, :, span] = (weight * abt(values, grads[head, span, :])).astype(
                    jnp.bfloat16
                )
        for head in range(local_heads):
            base = head * 3 * head_size
            key = mixed_ref[rows, base + head_size : base + 2 * head_size]
            turned = key.astype(jnp.float32).T.astype(jnp.bfloat16)
            value_grad = ab(weights[head], grads[head])
            key_grad = ab(score_grads[head], mixed_ref[:, base : base + head_size])
            query_grads[head] += ab(turned, score_grads[head])
            mixed_grad_ref[rows, base + head_size : base + 3 * head_size] = jnp.concatenate(
                [key_grad * scale, value_grad[:, :head_size]], axis=1
            ).astype(jnp.bfloat16)

        @pl.when(step == pl.num_programs(0) - 1)
        def _():
            for head in range(local_heads):
                base = head * 3 * head_size
                mixed_grad_ref[:, base : base + head_size] = (query_grads[head] * scale).T.astype(
                    jnp.bfloat16
                )

    return call(
        kernel,
        "attention_back",
        [mixed, queries, outs, grads],
        [bf16(*mixed.shape)],
        flops,
        grid=(length // block,),
        specs={number: pl.BlockSpec(memory_space=pl.ANY) for number in range(4)},
        scratch=[
            pltpu.VMEM((local_heads, length, 2 * head_size), jnp.bfloat16),
            pltpu.VMEM((local_heads, head_size, length), jnp.float32),
            pltpu.VMEM((local_heads, block, length), jnp.bfloat16),
            pltpu.VMEM((local_heads, block, length), jnp.bfloat16),
        ]
        + [pltpu.VMEM(array.shape, array.dtype) for array in (mixed, queries, outs, grads)]
        + [pltpu.SemaphoreType.DMA((4,))],
    )[0]


def project(stream, gains, biases, w_qkv, layer, per):
    tokens, width = stream.shape
    columns = w_qkv.shape[2] // per

    def kernel(stream_ref, gain_ref, bias_ref, weight_ref, mixed_ref, normed_ref):
        hat, unused = normalize(stream_ref[...].astype(jnp.float32))
        normed = (hat * gain_ref[layer : layer + 1] + bias_ref[layer : layer + 1]).astype(
            jnp.bfloat16
        )
        normed_ref[...] = normed
        for part in range(per):
            mixed_ref[part] = ab(
                normed, weight_ref[:, part * columns : (part + 1) * columns]
            ).astype(jnp.bfloat16)

    return call(
        kernel,
        "project",
        [stream, gains, biases, w_qkv],
        [bf16(per, tokens, columns), bf16(tokens, width)],
        2 * tokens * width * w_qkv.shape[2],
        specs={3: layer_spec(w_qkv, layer)},
    )


def middle_forward(
    me, images, parts, start, w_out, b_out, mlp_gain, mlp_bias, w_up, b_up, w_down, b_down, gains,
    biases, w_qkv,
):
    per, tokens, out_columns = parts.shape
    patches = tokens // images
    width = start.shape[1]
    hidden_width = w_up.shape[1]
    columns = w_qkv.shape[2] // per
    chunk = hidden_width // 2

    def kernel(
        me_ref, parts_ref, start_ref, w_out_ref, b_out_ref, mlp_gain_ref, mlp_bias_ref, w_up_ref,
        b_up_ref, w_down_ref, b_down_ref, gain_ref, bias_ref, weight_ref,
        first_ref, mlp_normed_ref, act_ref, slope_ref, second_ref, normed_ref, mixed_ref,
        *piece_refs,
    ):
        attended = jnp.concatenate([parts_ref[part] for part in range(per)], axis=1)
        first = start_ref[...].astype(jnp.float32) + ab(attended, w_out_ref[...]) + b_out_ref[0:1]
        first_ref[...] = first
        hat, unused = normalize(first)
        mlp_normed = (hat * mlp_gain_ref[...] + mlp_bias_ref[...]).astype(jnp.bfloat16)
        mlp_normed_ref[...] = mlp_normed
        second = first + b_down_ref[...]
        for piece in range(hidden_width // chunk):
            span = slice(piece * chunk, (piece + 1) * chunk)
            act, slope = gelu_parts(ab(mlp_normed, w_up_ref[:, span]) + b_up_ref[:, span])
            act = act.astype(jnp.bfloat16)
            act_ref[:, span] = act
            slope_ref[:, span] = slope.astype(jnp.bfloat16)
            second += ab(act, w_down_ref[span, :])
        second_ref[...] = second
        for shift, piece_ref in enumerate(piece_refs):
            rows = block_at(ahead(me_ref[0], shift, images), patches)
            piece_ref[...] = second_ref[rows, :].astype(jnp.bfloat16)
        hat, unused = normalize(second)
        normed = (hat * gain_ref[1:2] + bias_ref[1:2]).astype(jnp.bfloat16)
        normed_ref[...] = normed
        for part in range(per):
            mixed_ref[part] = ab(
                normed, weight_ref[:, part * columns : (part + 1) * columns]
            ).astype(jnp.bfloat16)

    return call(
        kernel,
        "middle_forward",
        [
            me, parts, start, w_out, b_out, mlp_gain, mlp_bias, w_up, b_up, w_down, b_down, gains,
            biases, w_qkv,
        ],
        [
            f32(tokens, width),
            bf16(tokens, width),
            bf16(tokens, hidden_width),
            bf16(tokens, hidden_width),
            f32(tokens, width),
            bf16(tokens, width),
            bf16(per, tokens, columns),
        ]
        + [bf16(patches, width)] * images,
        2 * tokens * width * (width + 2 * hidden_width + w_qkv.shape[2]),
        specs={3: layer_spec(w_out, 0), 13: layer_spec(w_qkv, 1)},
    )


def middle_back(
    me, grad_parts, pieces, second, first, slope, gains, mlp_gain, w_qkv, w_down, w_up, w_out
):
    per, tokens, columns = grad_parts.shape
    width = second.shape[1]
    hidden_width = w_up.shape[1]
    out_columns = width // per
    chunk = hidden_width // 2
    images = len(pieces)
    patches = tokens // images

    def kernel(
        me_ref, parts_ref, second_ref, first_ref, slope_ref, gain_ref, mlp_gain_ref, weight_ref,
        w_down_ref, w_up_ref, w_out_ref, *refs,
    ):
        piece_refs = refs[:images]
        (
            sent_ref, first_grad_ref, branch_ref, down_grad_ref, hidden_grad_ref, sums_ref,
            up_sum_ref, upper_ref,
        ) = refs[images:]
        for shift, piece_ref in enumerate(piece_refs):
            rows = block_at(ahead(me_ref[0], images - shift, images), patches)
            upper_ref[rows, :] = piece_ref[...]
        normed_grad = jnp.zeros((tokens, width), jnp.float32)
        for part in range(per):
            normed_grad += abt(
                parts_ref[part], weight_ref[:, part * columns : (part + 1) * columns]
            )
        back, gain_grad, bias_grad = norm_back(second_ref[...], gain_ref[1:2], normed_grad)
        second_grad = upper_ref[...].astype(jnp.float32) + back
        down_grad = second_grad.astype(jnp.bfloat16)
        down_grad_ref[...] = down_grad
        normed_grad = jnp.zeros((tokens, width), jnp.float32)
        for piece in range(hidden_width // chunk):
            span = slice(piece * chunk, (piece + 1) * chunk)
            hidden_grad = (
                abt(down_grad, w_down_ref[span, :]) * slope_ref[:, span].astype(jnp.float32)
            ).astype(jnp.bfloat16)
            hidden_grad_ref[:, span] = hidden_grad
            up_sum_ref[:, span] = jnp.sum(
                hidden_grad.astype(jnp.float32), axis=0, keepdims=True
            )
            normed_grad += abt(hidden_grad, w_up_ref[:, span])
        back, mlp_gain_grad, mlp_bias_grad = norm_back(
            first_ref[...], mlp_gain_ref[...], normed_grad
        )
        first_grad = second_grad + back
        first_grad_ref[...] = first_grad
        branch = first_grad.astype(jnp.bfloat16)
        branch_ref[...] = branch
        for part in range(per):
            sent_ref[part] = abt(
                branch, w_out_ref[part * out_columns : (part + 1) * out_columns, :]
            ).astype(jnp.bfloat16)
        row = lambda array: jnp.sum(array.astype(jnp.float32), axis=0, keepdims=True)
        sums = [gain_grad, bias_grad, mlp_gain_grad, mlp_bias_grad, row(down_grad), row(branch)]
        sums_ref[...] = jnp.concatenate(sums + [jnp.zeros((2, width), jnp.float32)], axis=0)

    return call(
        kernel,
        "middle_back",
        [
            me, grad_parts, second, first, slope, gains, mlp_gain, w_qkv, w_down, w_up, w_out,
        ]
        + list(pieces),
        [
            bf16(per, tokens, out_columns),
            f32(tokens, width),
            bf16(tokens, width),
            bf16(tokens, width),
            bf16(tokens, hidden_width),
            f32(8, width),
            f32(1, hidden_width),
        ],
        2 * tokens * width * (width + 2 * hidden_width + w_qkv.shape[2]),
        specs={7: layer_spec(w_qkv, 1), 10: layer_spec(w_out, 0)},
        scratch=[pltpu.VMEM((tokens, width), jnp.bfloat16)],
    )


def final_back(me, images, grad_parts, first_grad, start, gains, w_qkv):
    per, tokens, columns = grad_parts.shape
    width = start.shape[1]
    patches = tokens // images

    def kernel(
        me_ref, parts_ref, first_grad_ref, start_ref, gain_ref, weight_ref, sums_ref, *refs
    ):
        piece_refs, grad_ref = refs[:images], refs[images]
        normed_grad = jnp.zeros((tokens, width), jnp.float32)
        for part in range(per):
            normed_grad += abt(
                parts_ref[part], weight_ref[:, part * columns : (part + 1) * columns]
            )
        back, gain_grad, bias_grad = norm_back(
            start_ref[...].astype(jnp.float32), gain_ref[0:1], normed_grad
        )
        grad_ref[...] = (first_grad_ref[...] + back).astype(jnp.bfloat16)
        for shift, piece_ref in enumerate(piece_refs):
            piece_ref[...] = grad_ref[block_at(ahead(me_ref[0], shift, images), patches), :]
        sums_ref[...] = jnp.concatenate(
            [gain_grad, bias_grad, jnp.zeros((6, width), jnp.float32)], axis=0
        )

    return call(
        kernel,
        "final_back",
        [me, grad_parts, first_grad, start, gains, w_qkv],
        [f32(8, width)] + [bf16(patches, width)] * images,
        2 * tokens * width * w_qkv.shape[2],
        specs={5: layer_spec(w_qkv, 0)},
        scratch=[pltpu.VMEM((tokens, width), jnp.bfloat16)],
    )


def gather_pieces(me, pieces):
    images = len(pieces)
    patches, width = pieces[0].shape

    def kernel(me_ref, *refs):
        for shift in range(images):
            place = ahead(me_ref[0], images - shift, images)
            refs[images][place] = refs[shift][...].astype(jnp.float32)

    return call(
        kernel, "gather_pieces", [me] + list(pieces), [f32(images, patches, width)], 1
    )[0]


def side_by_side(parts_ref):
    return jnp.concatenate([parts_ref[part] for part in range(parts_ref.shape[0])], axis=1)


def weight_grads(
    normed1, grad_parts1, mlp_normed, hidden_grad, act, down_grad, attended1, branch1, parts0,
    branch0,
):
    tokens, width = normed1.shape
    hidden_width = act.shape[1]
    columns = grad_parts1.shape[0] * grad_parts1.shape[2]

    def kernel(
        normed_ref, grad_ref, mlp_normed_ref, hidden_grad_ref, act_ref, down_grad_ref,
        attended_ref, branch1_ref, parts_ref, branch0_ref, qkv_ref, up_ref, down_ref, out_ref,
    ):
        turned = mlp_normed_ref[...].T
        for block in range(hidden_width // width):
            span = slice(block * width, (block + 1) * width)
            up_ref[:, span] = ab(turned, hidden_grad_ref[:, span]).astype(jnp.bfloat16)
            down_ref[span, :] = ab(act_ref[:, span].T, down_grad_ref[...]).astype(jnp.bfloat16)
        turned = normed_ref[...].T
        for part in range(grad_ref.shape[0]):
            span = slice(part * grad_ref.shape[2], (part + 1) * grad_ref.shape[2])
            qkv_ref[:, span] = ab(turned, grad_ref[part]).astype(jnp.bfloat16)
        out_ref[0] = ab(side_by_side(parts_ref).T, branch0_ref[...]).astype(jnp.bfloat16)
        out_ref[1] = ab(attended_ref[...].T, branch1_ref[...]).astype(jnp.bfloat16)

    return call(
        kernel,
        "weight_grads",
        [
            normed1, grad_parts1, mlp_normed, hidden_grad, act, down_grad, attended1, branch1,
            parts0, branch0,
        ],
        [
            bf16(width, columns),
            bf16(width, hidden_width),
            bf16(hidden_width, width),
            bf16(2, width, width),
        ],
        2 * tokens * width * (columns + 2 * hidden_width + 2 * width),
    )


def last_grads(normed0, grad_parts0, out_grads, small):
    tokens, width = normed0.shape
    rows = small.shape[0]

    def kernel(normed_ref, grad_ref, out_grad_ref, small_ref, rows_ref):
        turned = normed_ref[...].T
        mixed_grad = side_by_side(grad_ref)
        for block in range(3):
            span = slice(block * width, (block + 1) * width)
            rows_ref[span, :] = ab(turned, mixed_grad[:, span]).astype(jnp.bfloat16)
        for block in range(2):
            rows_ref[(3 + block) * width : (4 + block) * width, :] = out_grad_ref[block]
        rows_ref[5 * width :, :] = small_ref[...]

    return call(
        kernel,
        "last_grads",
        [normed0, grad_parts0, out_grads, small],
        [bf16(5 * width + rows, width)],
        2 * tokens * width * width * 3,
    )[0]


def finish(up, down, qkv1, rows):
    width, hidden_width = up.shape
    steps = 4
    band = width // steps

    def kernel(up_ref, down_ref, qkv1_ref, *refs):
        blocks = refs[:5]
        up_out, down_out, qkv_out, proj_out = refs[5:]
        up_out[...] = up_ref[...].astype(jnp.float32)
        down_out[...] = down_ref[...].astype(jnp.float32)
        for block in range(3):
            qkv_out[0, :, block * width : (block + 1) * width] = blocks[block][...].astype(
                jnp.float32
            )
        qkv_out[1] = qkv1_ref[...].astype(jnp.float32)
        proj_out[0] = blocks[3][...].astype(jnp.float32)
        proj_out[1] = blocks[4][...].astype(jnp.float32)

    row_band = lambda size, columns: pl.BlockSpec((size, columns), lambda step: (step, 0))
    block_band = lambda block: pl.BlockSpec((band, width), lambda step: (block * steps + step, 0))
    layers = lambda columns: pl.BlockSpec((2, band, columns), lambda step: (0, step, 0))
    specs = {
        0: row_band(band, hidden_width),
        1: row_band(hidden_width // steps, width),
        2: row_band(band, 3 * width),
    }
    for block in range(5):
        specs[3 + block] = block_band(block)
    return call(
        kernel,
        "finish",
        [up, down, qkv1] + [rows] * 5,
        [
            f32(width, hidden_width),
            f32(hidden_width, width),
            f32(2, width, 3 * width),
            f32(2, width, width),
        ],
        1,
        grid=(steps,),
        specs=specs,
        out_specs={
            0: specs[0],
            1: specs[1],
            2: layers(3 * width),
            3: layers(width),
        },
    )


def slot_rows_of(capacity):
    return (capacity + 3 + 7) // 8 * 8


def place_slots(priority, choices, capacity, experts, top):
    tokens, width = top.shape
    half = width // 2
    span = slot_rows_of(capacity)

    def kernel(row_ref, column_ref, choice_ref, top_ref, target_ref, count_ref, *slot_refs):
        earlier = (column_ref[...] < row_ref[...]).astype(jnp.bfloat16)
        expert = lax.broadcasted_iota(jnp.int32, (experts, tokens), 0)
        picks = [(choice_ref[k : k + 1, :] == expert).astype(jnp.float32) for k in (0, 1)]
        before = [ab(pick.astype(jnp.bfloat16), earlier) for pick in picks]
        before[1] += jnp.sum(picks[0], axis=1, keepdims=True)
        targets = []
        hits = jnp.zeros((experts, 1), jnp.float32)
        for k in (0, 1):
            position = jnp.sum(before[k] * picks[k], axis=0, keepdims=True).astype(jnp.int32)
            kept = position < capacity
            targets.append(jnp.where(kept, choice_ref[k : k + 1, :] * span + position, -1))
            hits += jnp.sum(picks[k] * kept.astype(jnp.float32), axis=1, keepdims=True)
        misses = jnp.sum(picks[0] + picks[1], axis=1, keepdims=True) - hits
        target_ref[...] = jnp.concatenate(targets, axis=0)
        count_ref[...] = jnp.concatenate([hits, misses], axis=1)
        slot = lax.broadcasted_iota(jnp.int32, (experts * span, tokens), 0)
        taken = ((slot == targets[0]) | (slot == targets[1])).astype(jnp.bfloat16)
        for part, slots_ref in enumerate(slot_refs):
            slots_ref[...] = ab(taken, top_ref[:, part * half : (part + 1) * half]).astype(
                jnp.bfloat16
            )

    return call(
        kernel,
        "place_slots",
        [priority.reshape(1, tokens), priority.reshape(tokens, 1), choices.T, top],
        [
            jax.ShapeDtypeStruct((2, tokens), jnp.int32),
            f32(experts, 2),
            bf16(experts * span, half),
            bf16(experts * span, half),
        ],
        2 * tokens * experts * span * width,
    )


def upper_forward(
    me, parts, pieces, w_out, b_out, gain, bias, router_rows, targets, capacity
):
    blocks, patches, out_columns = parts.shape
    images = len(pieces)
    per = blocks // images
    tokens, width = images * patches, pieces[0].shape[1]
    experts = router_rows.shape[0]
    span = slot_rows_of(capacity)

    def kernel(
        me_ref, parts_ref, w_out_ref, b_out_ref, gain_ref, bias_ref, router_ref, target_ref, *refs
    ):
        piece_refs = refs[:images]
        upper_ref, normed_ref, gate_ref, slots_ref, attended_ref = refs[images:]
        for shift, piece_ref in enumerate(piece_refs):
            rows = block_at(ahead(me_ref[0], images - shift, images), patches)
            upper_ref[rows, :] = piece_ref[...].astype(jnp.float32)
        for image in range(images):
            attended_ref[image * patches : (image + 1) * patches, :] = jnp.concatenate(
                [parts_ref[image * per + part] for part in range(per)], axis=1
            )
        upper = upper_ref[...] + ab(attended_ref[...], w_out_ref[...]) + b_out_ref[1:2]
        upper_ref[...] = upper
        hat, unused = normalize(upper)
        normed = (hat * gain_ref[...] + bias_ref[...]).astype(jnp.bfloat16)
        normed_ref[...] = normed
        logits = abt(router_ref[...], normed)
        weights = jnp.exp(logits - jnp.max(logits, axis=0, keepdims=True))
        gates = weights / jnp.sum(weights, axis=0, keepdims=True)
        gate_ref[...] = gates
        digits = [digit.astype(jnp.float32) for digit in split3(gates)]
        row = lax.broadcasted_iota(jnp.int32, (span, width), 0)
        for expert in range(experts):
            slot = lax.broadcasted_iota(jnp.int32, (span, tokens), 0) + expert * span
            taken = (slot == target_ref[0:1, :]) | (slot == target_ref[1:2, :])
            taken = taken.astype(jnp.bfloat16)
            slots = ab(taken, normed)
            digit = jnp.concatenate(
                [digits[place][expert : expert + 1] for place in range(3)]
                + [jnp.zeros((5, tokens), jnp.float32)],
                axis=0,
            ).astype(jnp.bfloat16)
            scalars = abt(digit, taken)
            scalars = jnp.concatenate(
                [scalars, jnp.zeros((8, width - span), jnp.float32)], axis=1
            )
            for place in range(3):
                slots = jnp.where(row == capacity + place, scalars[place : place + 1], slots)
            slots_ref[expert] = slots.astype(jnp.bfloat16)

    return call(
        kernel,
        "upper_forward",
        [me, parts, w_out, b_out, gain, bias, router_rows, targets] + list(pieces),
        [
            f32(tokens, width),
            bf16(tokens, width),
            f32(experts, tokens),
            bf16(experts, span, width),
            bf16(tokens, width),
        ],
        2 * tokens * width * (width + experts * span),
        specs={2: layer_spec(w_out, 1)},
    )


def expert_core(rows, tops, up, up_bias, down, down_bias, capacity):
    groups, span, width = rows.shape
    total = groups * span
    hidden_width = up.shape[2]
    steps = 2
    chunk = hidden_width // steps

    def kernel(
        rows_ref, left_ref, right_ref, up_ref, up_bias_ref, down_ref, down_bias_ref,
        act_ref, hidden_grad_ref, out_grad_ref, rows_grad_ref, up_sum_ref, down_sum_ref,
        gate, gate_grad, rows_grad, top_ref,
    ):
        step = pl.program_id(0)

        @pl.when(step == 0)
        def _():
            lane = lax.broadcasted_iota(jnp.int32, (span, width), 1)
            row = lax.broadcasted_iota(jnp.int32, (span, width), 0)
            for group in range(groups):
                some = slice(group * span, (group + 1) * span)
                values = rows_ref[some, :].astype(jnp.float32)
                scalars = (
                    values[capacity : capacity + 1]
                    + values[capacity + 1 : capacity + 2]
                    + values[capacity + 2 : capacity + 3]
                )
                column = jnp.sum(jnp.where(lane == row, scalars, 0.0), axis=1, keepdims=True)
                gate[some, :] = jnp.where(row[:, :1] < capacity, column, 0.0)
            top_ref[:, : width // 2] = left_ref[...]
            top_ref[:, width // 2 :] = right_ref[...]
            top_rows = top_ref[...].astype(jnp.float32)
            out_grad = (gate[...] * top_rows).astype(jnp.bfloat16)
            out_grad_ref[...] = out_grad
            down_sum_ref[...] = jnp.sum(out_grad.astype(jnp.float32), axis=0, keepdims=True)
            gate_grad[...] = jnp.sum(top_rows * down_bias_ref[...], axis=1, keepdims=True)
            rows_grad[...] = jnp.zeros_like(rows_grad)

        up_piece = up_ref[...]
        act, slope = gelu_parts(ab(rows_ref[...], up_piece) + up_bias_ref[...])
        act = act.astype(jnp.bfloat16)
        act_ref[...] = act
        plain = abt(top_ref[...], down_ref[...])
        gate_grad[...] += jnp.sum(act.astype(jnp.float32) * plain, axis=1, keepdims=True)
        hidden_grad = (gate[...] * plain * slope).astype(jnp.bfloat16)
        hidden_grad_ref[...] = hidden_grad
        up_sum_ref[...] = jnp.sum(hidden_grad.astype(jnp.float32), axis=0, keepdims=True)
        rows_grad[...] += abt(hidden_grad, up_piece)

        @pl.when(step == steps - 1)
        def _():
            lane = lax.broadcasted_iota(jnp.int32, (span, width), 1)
            row = lax.broadcasted_iota(jnp.int32, (span, width), 0)
            for group in range(groups):
                some = slice(group * span, (group + 1) * span)
                scalars = jnp.sum(
                    jnp.where((lane == row) & (row < capacity), gate_grad[some, :], 0.0),
                    axis=0,
                    keepdims=True,
                )
                values = rows_grad[some, :]
                for place, digit in enumerate(split3(scalars)):
                    values = jnp.where(
                        row == capacity + place, digit.astype(jnp.float32), values
                    )
                rows_grad[some, :] = values
            rows_grad_ref[...] = rows_grad[...].astype(jnp.bfloat16)

    column_block = lambda rows_of: pl.BlockSpec((rows_of, chunk), lambda step: (0, step))
    return call(
        kernel,
        "expert_core",
        [rows.reshape(total, width)]
        + [top.reshape(total, width // 2) for top in tops]
        + [up, up_bias, down, down_bias],
        [
            bf16(total, hidden_width),
            bf16(total, hidden_width),
            bf16(total, width),
            bf16(total, width),
            f32(1, hidden_width),
            f32(1, width),
        ],
        6 * total * width * hidden_width,
        grid=(steps,),
        specs={
            3: pl.BlockSpec((None, width, chunk), lambda step: (0, 0, step)),
            4: column_block(1),
            5: pl.BlockSpec((None, chunk, width), lambda step: (0, step, 0)),
        },
        out_specs={0: column_block(total), 1: column_block(total), 4: column_block(1)},
        scratch=[
            pltpu.VMEM((total, 1), jnp.float32),
            pltpu.VMEM((total, 1), jnp.float32),
            pltpu.VMEM((total, width), jnp.float32),
            pltpu.VMEM((total, width), jnp.bfloat16),
        ],
    )


def upper_back(
    me, slot_grads, targets, target_columns, gates, normed, upper, top, gain, router_rows, w_out,
    capacity, images, per,
):
    experts, span, width = slot_grads.shape
    tokens = normed.shape[0]
    patches = tokens // images
    out_columns = width // per

    def kernel(
        me_ref, slot_ref, target_ref, column_ref, gate_ref, normed_ref, upper_ref, top_ref,
        gain_ref, router_ref, w_out_ref,
        attended_grad_ref, branch_ref, router_grad_ref, sums_ref, *piece_refs,
    ):
        slot = lax.broadcasted_iota(jnp.int32, (tokens, experts * span), 1)
        taken = (slot == column_ref[:, 0:1]) | (slot == column_ref[:, 1:2])
        normed_grad = ab(taken.astype(jnp.bfloat16), slot_ref[...])
        gates_grad = []
        for expert in range(experts):
            scalars = slot_ref[expert * span : (expert + 1) * span, :].astype(jnp.float32)
            scalars = scalars[capacity : capacity + 3, :span]
            scalars = jnp.concatenate(
                [scalars, jnp.zeros((5, span), jnp.float32)], axis=0
            ).astype(jnp.bfloat16)
            place = lax.broadcasted_iota(jnp.int32, (span, tokens), 0) + expert * span
            here = (place == target_ref[0:1, :]) | (place == target_ref[1:2, :])
            spread = ab(scalars, here.astype(jnp.bfloat16))
            gates_grad.append(jnp.sum(spread, axis=0, keepdims=True))
        gates_grad = jnp.concatenate(gates_grad, axis=0)
        gates = gate_ref[...]
        logit_grad = gates * (gates_grad - jnp.sum(gates_grad * gates, axis=0, keepdims=True))
        logit_grad = logit_grad.astype(jnp.bfloat16)
        router_grad_ref[...] = ab(logit_grad, normed_ref[...])
        normed_grad += atb(logit_grad, router_ref[...])
        back, gain_grad, bias_grad = norm_back(upper_ref[...], gain_ref[...], normed_grad)
        branch = (back + top_ref[...].astype(jnp.float32)).astype(jnp.bfloat16)
        branch_ref[...] = branch
        for shift, piece_ref in enumerate(piece_refs):
            piece_ref[...] = branch_ref[block_at(ahead(me_ref[0], shift, images), patches), :]
        attended_grad = abt(branch, w_out_ref[...]).astype(jnp.bfloat16)
        for image in range(images):
            for part in range(per):
                attended_grad_ref[image * per + part] = attended_grad[
                    image * patches : (image + 1) * patches,
                    part * out_columns : (part + 1) * out_columns,
                ]
        shift = jnp.sum(branch.astype(jnp.float32), axis=0, keepdims=True)
        sums_ref[...] = jnp.concatenate(
            [gain_grad, bias_grad, shift, jnp.zeros((5, width), jnp.float32)], axis=0
        )

    return call(
        kernel,
        "upper_back",
        [
            me, slot_grads.reshape(experts * span, width), targets, target_columns, gates, normed,
            upper, top, gain, router_rows, w_out,
        ],
        [
            bf16(images * per, patches, out_columns),
            bf16(tokens, width),
            f32(experts, width),
            f32(8, width),
        ]
        + [bf16(patches, width)] * images,
        2 * tokens * width * (width + experts * span),
        specs={10: layer_spec(w_out, 1)},
    )


def combine(table, target_columns, choices, gates, upper):
    experts, span, width = table.shape
    tokens = upper.shape[0]

    def kernel(table_ref, column_ref, choice_ref, gate_ref, upper_ref, out_ref):
        gates = gate_ref[...].T
        total = upper_ref[...]
        slot = lax.broadcasted_iota(jnp.int32, (tokens, experts * span), 1)
        expert = lax.broadcasted_iota(jnp.int32, (tokens, experts), 1)
        for k in (0, 1):
            taken = (slot == column_ref[:, k : k + 1]).astype(jnp.bfloat16)
            gate = jnp.sum(
                jnp.where(expert == choice_ref[:, k : k + 1], gates, 0.0), axis=1, keepdims=True
            )
            total += gate * ab(taken, table_ref[...])
        out_ref[...] = total.astype(jnp.bfloat16)

    return call(
        kernel,
        "combine",
        [table.reshape(experts * span, width), target_columns, choices, gates, upper],
        [bf16(tokens, width)],
        4 * tokens * width * experts * span,
    )[0]


def plane_groups(blocks, images):
    per = blocks // images
    return [[row * per + column for column in range(per)] for row in range(images)]


def line_groups(blocks, images):
    per = blocks // images
    return [[row * per + column for row in range(images)] for column in range(per)]


def swap(array, groups=None):
    return lax.all_to_all(
        array, "blk", split_axis=0, concat_axis=0, tiled=True, axis_index_groups=groups
    )


def tie(*arrays):
    return lax.optimization_barrier(arrays)


def sum_all(array, plane, line):
    width = array.shape[1]
    stages = (("dp", None), ("blk", plane), ("blk", line))

    def count(axis, groups):
        return lax.axis_size(axis) if groups is None else len(groups[0])

    for axis, groups in stages:
        parts = array.reshape(count(axis, groups), -1, width)
        parts = lax.all_to_all(parts, axis, 0, 0, tiled=True, axis_index_groups=groups)
        array = jnp.sum(parts.astype(jnp.float32), axis=0).astype(jnp.bfloat16)
    for axis, groups in reversed(stages):
        parts = jnp.broadcast_to(array[None], (count(axis, groups),) + array.shape)
        parts = lax.all_to_all(parts, axis, 0, 0, tiled=True, axis_index_groups=groups)
        array = parts.reshape(-1, width)
    return array


def send_ahead(pieces, groups):
    out = [pieces[0]]
    for shift in range(1, len(pieces)):
        pairs = [
            (member, group[(place + shift) % len(group)])
            for group in groups
            for place, member in enumerate(group)
        ]
        out.append(lax.ppermute(pieces[shift], "blk", pairs))
    return out


def count_bits(counts, width):
    bits = (counts.reshape(-1)[:, None].astype(jnp.int32) >> jnp.arange(10, dtype=jnp.int32)) & 1
    flat = bits.reshape(-1).astype(jnp.float32)
    return jnp.pad(flat, (0, -flat.size % width)).reshape(-1, width)


def count_sums(rows, number):
    bits = rows.reshape(-1)[: number * 10].reshape(number, 10).astype(jnp.float32)
    return jnp.sum(bits * (2.0 ** jnp.arange(10)), axis=1).astype(jnp.int32)


def per_device(
    tokens,
    attn_gain,
    attn_bias,
    w_qkv,
    w_out,
    b_out,
    mlp_gain,
    mlp_bias,
    w_up,
    b_up,
    w_down,
    b_down,
    moe_gain,
    moe_bias,
    router,
    expert_up,
    expert_up_bias,
    expert_down,
    expert_down_bias,
    priority,
    routes,
    out_grad,
):
    images, patches, width = tokens.shape
    tok_count = images * patches
    blocks = lax.axis_size("blk")
    per = blocks // images
    local_heads = HEADS // per
    head_size = width // HEADS
    plane = plane_groups(blocks, images)
    line = line_groups(blocks, images)
    experts = router.shape[1]
    capacity = (21 * tok_count + 10 * experts - 1) // (10 * experts)
    span = slot_rows_of(capacity)
    row = lambda vector: vector.reshape(1, -1)
    me = (lax.axis_index("blk") // per).astype(jnp.int32).reshape(1)
    router_rows = router.T
    choices = routes.reshape(tok_count, 2)
    top = out_grad.reshape(tok_count, width)

    start = swap(tokens, line).reshape(tok_count, width)

    targets, counts, left_slots, right_slots = place_slots(
        priority, choices, capacity, experts, top
    )
    target_columns = targets.T
    start, left_slots, target_columns = tie(start, left_slots, target_columns)

    mixed0, normed0 = project(start, attn_gain, attn_bias, w_qkv, 0, per)
    arrived0 = swap(mixed0, plane).reshape(blocks * patches, -1)
    arrived0, left_slots = tie(arrived0, left_slots)
    left_top = swap(left_slots.reshape(experts, span, width // 2))
    out0, plain0, queries0 = attention(arrived0, head_size, local_heads, None)
    out0, left_top = tie(out0, left_top)
    parts0 = swap(out0.reshape(per, tok_count, -1), plane)

    parts0, right_slots = tie(parts0, right_slots)
    right_top = swap(right_slots.reshape(experts, span, width // 2))
    first, mlp_normed, act, slope, second, normed1, mixed1, *pieces = middle_forward(
        me, images, parts0, start, w_out, b_out, row(mlp_gain), row(mlp_bias), w_up, row(b_up),
        w_down, row(b_down), attn_gain, attn_bias, w_qkv,
    )
    mixed1, right_top = tie(mixed1, right_top)
    arrived1 = swap(mixed1, plane).reshape(blocks * patches, -1)
    pieces = send_ahead(pieces, line)
    out1, plain1, queries1 = attention(arrived1, head_size, local_heads, (images, per))
    out1, *pieces = tie(out1, *pieces)
    parts1 = swap(out1.reshape(blocks, patches, -1))

    upper, moe_normed, gates, slots, attended1 = upper_forward(
        me, parts1, pieces, w_out, b_out, row(moe_gain), row(moe_bias), router_rows, targets,
        capacity,
    )
    expert_rows = swap(slots)
    expert_act, hidden_grad, out_rows_grad, rows_grad, up_bias_sum, down_bias_sum = expert_core(
        expert_rows, (left_top, right_top), expert_up, expert_up_bias, expert_down, expert_down_bias, capacity
    )
    slot_grads = swap(rows_grad.reshape(blocks, span, width))
    expert_result = (
        jnp.dot(expert_act, expert_down[0], preferred_element_type=jnp.float32) + expert_down_bias
    ).astype(jnp.bfloat16)
    down_sum = jnp.einsum(
        "rf,rd->fd", expert_act, out_rows_grad, preferred_element_type=jnp.float32
    ).astype(jnp.bfloat16)
    up_sum = jnp.einsum(
        "rd,rf->df",
        expert_rows.reshape(blocks * span, width),
        hidden_grad,
        preferred_element_type=jnp.float32,
    ).astype(jnp.bfloat16)
    slot_grads, expert_result, down_sum, up_sum = tie(slot_grads, expert_result, down_sum, up_sum)
    sent1, upper_branch, router_sum, upper_sums, *pieces = upper_back(
        me, slot_grads, targets, target_columns, gates, moe_normed, upper, top, row(moe_gain),
        router_rows, w_out, capacity, images, per,
    )
    expert_sums = [
        lax.psum_scatter(part.astype(jnp.bfloat16), "dp", scatter_dimension=1, tiled=True).astype(
            jnp.float32
        )
        for part in (up_sum[None], up_bias_sum, down_sum[None], down_bias_sum)
    ]

    grads1 = swap(sent1).reshape(blocks * patches, -1)
    pieces = send_ahead(pieces, line)
    grads1, expert_result = tie(grads1, expert_result)
    table = swap(expert_result.reshape(blocks, span, width))
    mixed_grad1 = attention_back(
        arrived1, queries1, plain1, grads1, head_size, local_heads, (images, per),
        40 * head_size * local_heads * (blocks * patches) ** 2,
    )
    mixed_grad1, table, *pieces = tie(mixed_grad1, table, *pieces)
    grad_parts1 = swap(mixed_grad1.reshape(per, tok_count, -1), plane)
    grad_parts1, *expert_sums = tie(grad_parts1, *expert_sums)

    sent0, first_grad, first_branch, down_grad, mlp_hidden_grad, middle_sums, up_bias_row = (
        middle_back(
            me, grad_parts1, pieces, second, first, slope, attn_gain,
            row(mlp_gain), w_qkv, w_down, w_up, w_out,
        )
    )
    grads0 = swap(sent0, plane).reshape(blocks * patches, -1)
    second_qkv, up_weight_sum, down_weight_sum, out_grads = weight_grads(
        normed1, grad_parts1, mlp_normed, mlp_hidden_grad, act, down_grad, attended1,
        upper_branch, parts0, first_branch,
    )
    grads0, second_qkv = tie(grads0, second_qkv)
    second_qkv, up_weight_sum, down_weight_sum = lax.psum(
        (second_qkv, up_weight_sum, down_weight_sum), ("dp", "blk")
    )

    def last_part(step, carry):
        step, grads, projections, rows_of_slots = tie(step, grads0, out_grads, table)
        mixed_grad0 = attention_back(
            arrived0, queries0, plain0, grads, head_size, local_heads, None, 1
        )
        grad_parts0 = swap(mixed_grad0.reshape(per, tok_count, -1), plane)
        final = combine(rows_of_slots, target_columns, choices, gates, upper)
        first_sums, *pieces = final_back(
            me, images, grad_parts0, first_grad, start, attn_gain, w_qkv
        )
        pieces = send_ahead(pieces, line)
        small = jnp.concatenate(
            [
                upper_sums[0:3],
                middle_sums[0:6],
                first_sums[0:2],
                up_bias_row.reshape(-1, width),
                router_sum,
                count_bits(counts, width),
            ]
        )
        small = jnp.pad(small, ((0, small_rows - small.shape[0]), (0, 0))).astype(jnp.bfloat16)
        rows = last_grads(normed0, grad_parts0, projections, small)
        rows = sum_all(rows, plane, line)
        return (rows, gather_pieces(me, pieces), final)

    devices = 8 * blocks * lax.axis_size("dp")
    small_rows = 11 + w_up.shape[1] // width + experts + -(-20 * experts // width)
    small_rows += -small_rows % devices
    trips = jnp.minimum(priority[0, 0], 0) + 1
    rows, start_group, final = lax.fori_loop(
        0,
        trips,
        last_part,
        (
            jnp.zeros((5 * width + small_rows, width), jnp.bfloat16),
            second.reshape(images, patches, width),
            upper_branch,
        ),
    )
    up_weight_sum, down_weight_sum, qkv_sum, proj_sum = finish(
        up_weight_sum, down_weight_sum, second_qkv, rows
    )
    hidden_rows = w_up.shape[1] // width
    wide = rows[5 * width :].astype(jnp.float32)
    router_at = 11 + hidden_rows
    count_rows = -(-20 * experts // width)
    bits = wide[router_at + experts : router_at + experts + count_rows]
    number = count_sums(bits, 2 * experts).reshape(experts, 2)
    return (
        final.reshape(images, patches, width),
        start_group,
        jnp.stack([wide[9], wide[3]]),
        jnp.stack([wide[10], wide[4]]),
        qkv_sum,
        proj_sum,
        jnp.stack([wide[8], wide[2]]),
        wide[5],
        wide[6],
        up_weight_sum,
        wide[11:router_at].reshape(-1),
        down_weight_sum,
        wide[7],
        wide[0],
        wide[1],
        wide[router_at : router_at + experts].T,
        expert_sums[0],
        expert_sums[1],
        expert_sums[2],
        expert_sums[3],
        number[:, 0],
        number[:, 1],
    )


def solution(mesh):
    return jax.shard_map(
        per_device,
        mesh=mesh,
        in_specs=(
            P("dp", "blk", None),
            P(),
            P(),
            P(),
            P(),
            P(),
            P(),
            P(),
            P(),
            P(),
            P(),
            P(),
            P(),
            P(),
            P(),
            P("blk", None, None),
            P("blk", None),
            P("blk", None, None),
            P("blk", None),
            P(("dp", "blk"), None),
            P("dp", "blk", None),
            P("dp", "blk", None),
        ),
        out_specs=(
            P("dp", "blk", None),
            P("dp", "blk", None),
            P(),
            P(),
            P(),
            P(),
            P(),
            P(),
            P(),
            P(),
            P(),
            P(),
            P(),
            P(),
            P(),
            P(),
            P("blk", "dp", None),
            P("blk", "dp"),
            P("blk", "dp", None),
            P("blk", "dp"),
            P(),
            P(),
        ),
        check_vma=False,
    )
```

time: 1090 us -> 556 us (0.51)
  waiting for transfers between devices: 426 us -> 83.1 us
  matrix products: 231 us -> 17.4 us
  Pallas kernels: 0 us -> 174 us
  local copies, waits for them, and re-layouts: 187 us -> 18.1 us
  blocking collectives: 48.4 us -> 158 us
  other arithmetic: 87.8 us -> 13.2 us
    psum x1, waiting for transfers between devices: 219 us -> 0.11 us  [per_device(): lax.psum((second_qkv, up_weight_sum, down_weight_sum), ('dp', 'blk'))]
    dot_general x83 -> x3, matrix products: 231 us -> 17.4 us  [the longest x1 7.08 us: per_device(): jnp.einsum('rd,rf->df', expert_rows.reshape(blocks * span, width), hidden...]
    pallas_call x0 -> x17, Pallas kernels: none -> 174 us  [call(): pl.pallas_call(kernel, grid=grid, in_specs=[specs.get(i, whole(array.shap...]
    all_to_all x0 -> x9, blocking collectives: none -> 158 us  [the longest x4 88.8 us: swap(): lax.all_to_all(array, 'blk', split_axis=0, concat_axis=0, tiled=True, axi...]
    all_to_all x12 -> x11, waiting for transfers between devices: 208 us -> 71.5 us  [the longest x10 67.3 us: swap(): lax.all_to_all(array, 'blk', split_axis=0, concat_axis=0, tiled=True, axi...]
    psum x1 -> x0, blocking collectives: 48.4 us -> none  [per_device(): lax.psum((first_gain, first_bias, first_qkv, first_proj, first_shift, sec...]
    unnamed x261 -> x33, local copies, waits for them, and re-layouts: 43.2 us -> 5.42 us
    reduce_sum x32 -> x4, other arithmetic: 35.6 us -> 2.59 us  [the longest x3 2.48 us: sum_all(): array = jnp.sum(parts.astype(jnp.float32), axis=0).astype(jnp.bfloat16)]
  transfers between devices with their start and end apart: 17 -> 25, of which waited for: 12 -> 14; matrix products, arithmetic and copies ran while one was open for 20% -> 9% of each run, Pallas kernels for 0% -> 23%
where the time goes in v1:
time: 556 us; the launch traced here: 548 us
  Pallas kernels  174 us (31%)
  blocking collectives  158 us (28%)
  waiting for transfers between devices  83.1 us (15%)
  starting transfers between devices  68.3 us (12%)
  local copies, waits for them, and re-layouts  18.1 us (3%)
  matrix products  17.4 us (3%)
  between operations  15.1 us (3%)
  other arithmetic  13.2 us (2%)
    pallas_call x17, Pallas kernels, call(): pl.pallas_call(kernel, grid=grid, in_specs=[specs.get(i, whole(array.shap...  174 us
    all_to_all x4, blocking collectives, swap(): lax.all_to_all(array, 'blk', split_axis=0, concat_axis=0, tiled=True, axi...  88.8 us
    all_to_all x5, blocking collectives, sum_all(): lax.all_to_all(parts, axis, 0, 0, tiled=True, axis_index_groups=groups)  69.6 us
    all_to_all x10, waiting for transfers between devices, swap(): lax.all_to_all(array, 'blk', split_axis=0, concat_axis=0, tiled=True, axi...  67.3 us
    all_to_all x10, starting transfers between devices, swap(): lax.all_to_all(array, 'blk', split_axis=0, concat_axis=0, tiled=True, axi...  48.9 us
    ppermute x9, starting transfers between devices, send_ahead(): out.append(lax.ppermute(pieces[shift], 'blk', pairs))  14.4 us
  transfers between devices with their start and end apart: 25, of which 14 were waited for; matrix products, arithmetic and copies ran while one was open for 9% of the time, Pallas kernels for 23%

profile of v1, /device:TPU:0, one launch (start us, length us, event | category | flops | bytes accessed | tf_op | source)
XLA Modules:
  0.0 547.5 jit_solution(10214256782306605383)
XLA Ops:
  7.2 6.6 %all-to-all-start.7 = ((bf16[4,128,512]{2,1,0:T(8,128)(2,1)}), bf16[4,128,512]{2,1,0:T(8,128)(2,1)}, u32[]{:S(2)}, u32[]{:S(2)}) async-start(bf16[4,128,512]{2,1,0:T(8,128)(2,1)} %param.24), calls=%async_computation.7 | async-start | bytes 1048576 | tf_op jit(solution)/shard_map/all_to_all | solution.py:966
  13.8 1.5 copy.56.column_ref
  15.3 3.3 place_slots.1
  19.4 9.0 %all-to-all-done.7 = bf16[4,128,512]{2,1,0:T(8,128)(2,1)} async-done(((bf16[4,128,512]{2,1,0:T(8,128)(2,1)}), bf16[4,128,512]{2,1,0:T(8,128)(2,1)}, u32[]{:S(2)}, u32[]{:S(2)}) %all-to-all-start.7) | async-done | bytes 524320 | tf_op jit(solution)/shard_map/all_to_all | solution.py:966
  28.4 3.7 project.1
  32.1 23.7 %all_to_all.138 = bf16[4,512,384]{2,1,0:T(8,128)(2,1)} all-to-all(bf16[4,512,384]{2,1,0:T(8,128)(2,1)} %get-tuple-element.486), channel_id=1, replica_groups={{0,1,2,3},{4,5,6,7},{8,9,10,11},{12,13,14,15},{16,17,18,19},{20,21,22,2..., dimensions={0} | all-to-all | bytes 3145728 | tf_op jit(solution)/shard_map/all_to_all | solution.py:966
  55.8 4.2 all-to-all-start.9
  60.0 14.1 %attention.2 = (bf16[2048,128]{1,0:T(8,128)(2,1)}, f32[2048,128]{1,0:T(8,128)}, bf16[2048,512]{1,0:T(8,128)(2,1)}) custom-call(bf16[2048,384]{1,0:T(8,128)(2,1)} %bitcast.93), custom_call_target="tpu_custom_call" | custom-call | flops 8589934592 | bytes 5242880 | tf_op jit(solution)/shard_map/attention/pallas_call | solution.py:79
  74.5 11.4 %all_to_all.139.parts_ref = bf16[4,512,128]{2,1,0:T(8,128)(2,1)} all-to-all(bf16[4,512,128]{2,1,0:T(8,128)(2,1)} %bitcast.111), channel_id=1, replica_groups={{0,1,2,3},{4,5,6,7},{8,9,10,11},{12,13,14,15},{16,17,18,19},{20,21,22,2..., dimensions={0} | all-to-all | bytes 1048576 | tf_op jit(solution)/shard_map/all_to_all | solution.py:966
  85.9 5.5 %all-to-all-start.11 = ((bf16[16,72,256]{2,1,0:T(8,128)(2,1)}), bf16[16,72,256]{2,1,0:T(8,128)(2,1)}, u32[]{:S(2)}, u32[]{:S(2)}) async-start(bf16[16,72,256]{2,1,0:T(8,128)(2,1)} %bitcast.108), calls=%async_computation.11 | async-start | bytes 1179648 | tf_op jit(solution)/shard_map/all_to_all | solution.py:966
  91.4 11.9 %middle_forward.1 = (f32[512,512]{1,0:T(8,128)}, bf16[512,512]{1,0:T(8,128)(2,1)}, bf16[512,2048]{1,0:T(8,128)(2,1)}, bf16[512,2048]{1,0:T(8,128)(2,1)}, f32[512...) custom-call(s32[1]{0:T(128)} %bitcast.me_ref, ...), custom_call_target="tpu_custom_call" | custom-call | flops 3221225472 | bytes 18900996 | tf_op jit(solution)/shard_map/middle_forward/pallas_call | solution.py:79
  104.5 4.4 all-to-all-start.12
  110.3 1.8 collective-permute-start.4
  112.1 1.6 collective-permute-start.5
  113.7 9.9 %all-to-all-done.12 = bf16[4,512,384]{2,1,0:T(8,128)(2,1)} async-done(((bf16[4,512,384]{2,1,0:T(8,128)(2,1)}), bf16[4,512,384]{2,1,0:T(8,128)(2,1)}, u32[]{:S(2)}, u32[]{:S(2)}) %all-to-all-start.12) | async-done | bytes 1572896 | tf_op jit(solution)/shard_map/all_to_all | solution.py:966
  123.7 14.0 %attention.3 = (bf16[2048,128]{1,0:T(8,128)(2,1)}, f32[2048,128]{1,0:T(8,128)}, bf16[2048,512]{1,0:T(8,128)(2,1)}) custom-call(bf16[2048,384]{1,0:T(8,128)(2,1)} %bitcast.16.mixed_ref.mixed_hbm), custom_call_target="tpu_custom_call" | custom-call | flops 8589934592 | bytes 5242880 | tf_op jit(solution)/shard_map/attention/pallas_call | solution.py:79
  137.7 20.6 %all_to_all.140.parts_ref = bf16[16,128,128]{2,1,0:T(8,128)(2,1)} all-to-all(bf16[16,128,128]{2,1,0:T(8,128)(2,1)} %bitcast.110), channel_id=1, replica_groups=mesh['dp'=2,'blk'=16] {'blk'}, dimensions={0} | all-to-all | bytes 1048576 | tf_op jit(solution)/shard_map/all_to_all | solution.py:966
  158.3 5.1 upper_forward.1
  163.4 33.2 %all_to_all.141 = bf16[16,72,512]{2,1,0:T(8,128)(2,1)} all-to-all(bf16[16,72,512]{2,1,0:T(8,128)(2,1)} %get-tuple-element.508), channel_id=1, replica_groups=mesh['dp'=2,'blk'=16] {'blk'}, dimensions={0} | all-to-all | bytes 2359296 | tf_op jit(solution)/shard_map/all_to_all | solution.py:966
  196.6 20.0 %expert_core.1 = (bf16[1152,2048]{1,0:T(8,128)(2,1)}, bf16[1152,2048]{1,0:T(8,128)(2,1)}, bf16[1152,512]{1,0:T(8,128)(2,1)}, bf16[1152,512]{1,0:T(8,128)(2,1)}, f32[1,2048]{1,0:T(1,128)}, /*index=5*/f32[1,512]{1,0:T(1,128)}) custom-call(bf16[1152,512]{1,0:T(8,128)(2,1)} %bitcast.102, bf16[1152,256]{1,0:T(8,128)(2,1)} %bitcast.22.left_ref, ...), custom_call_target="tpu_custom_call" | custom-call | flops 7247757312 | bytes 18370560 | tf_op jit(solution)/shard_map/expert_core/pallas_call | solution.py:79
  216.6 4.4 all-to-all-start.15
  223.6 7.1 %convolution_convert_fusion = bf16[512,2048]{1,0:T(8,128)(2,1)} fusion(bf16[1152,512]{1,0:T(8,128)(2,1)} %bitcast.103, bf16[1152,2048]{1,0:T(8,128)(2,1)} %get-tuple-element.514), kind=kOutput, calls=%fused_computation.4 | convolution fusion | flops 2416967680 | bytes 7995392 | tf_op jit(solution)/shard_map/rd,rf->df/dot_general | solution.py:1101
  230.7 6.2 %fusion = bf16[1152,512]{1,0:T(8,128)(2,1)} fusion(bf16[1152,2048]{1,0:T(8,128)(2,1)} %get-tuple-element.512, bf16[1,2048,512]{2,1,0:T(8,128)(2,1)S(1)} %copy-done.17, f32[512]{0:T(512)S(1)} %bitcast.139), kind=kOutput, calls=%fused_computation.3 | convolution fusion | flops 2417098752 | bytes 7997440 | tf_op jit(solution)/shard_map/dot_general | solution.py:1096
  236.9 4.1 convolution_convert_fusion.1
  241.0 5.6 %all-to-all-done.15 = bf16[16,72,512]{2,1,0:T(8,128)(2,1)} async-done(((bf16[16,72,512]{2,1,0:T(8,128)(2,1)}), bf16[16,72,512]{2,1,0:T(8,128)(2,1)}, u32[]{:S(2)}, u32[]{:S(2)}) %all-to-all-start.15) | async-done | bytes 1179680 | tf_op jit(solution)/shard_map/all_to_all | solution.py:966
  246.6 5.6 %upper_back.1 = (bf16[16,128,128]{2,1,0:T(8,128)(2,1)}, bf16[512,512]{1,0:T(8,128)(2,1)}, f32[16,512]{1,0:T(8,128)}, f32[8,512]{1,0:T(8,128)}, bf16[128,512]{1,0...) custom-call(s32[1]{0:T(128)} %bitcast.me_ref, ...), custom_call_target="tpu_custom_call" | custom-call | flops 872415232 | bytes 6006788 | tf_op jit(solution)/shard_map/upper_back/pallas_call | solution.py:79
  252.2 6.2 %all-to-all-start.16 = ((bf16[16,128,128]{2,1,0:T(8,128)(2,1)}), bf16[16,128,128]{2,1,0:T(8,128)(2,1)}, u32[]{:S(2)}, u32[]{:S(2)}) async-start(bf16[16,128,128]{2,1,0:T(8,128)(2,1)} %get-tuple-element.523), calls=%async_computation.16 | async-start | bytes 1048576 | tf_op jit(solution)/shard_map/all_to_all | solution.py:966
  259.0 13.3 %all-to-all-done.16 = bf16[16,128,128]{2,1,0:T(8,128)(2,1)} async-done(((bf16[16,128,128]{2,1,0:T(8,128)(2,1)}), bf16[16,128,128]{2,1,0:T(8,128)(2,1)}, u32[]{:S(2)}, u32[]{:S(2)}) %all-to-all-start.16) | async-done | bytes 524320 | tf_op jit(solution)/shard_map/all_to_all | solution.py:966
  272.3 4.4 all-to-all-start.17
  276.7 1.8 collective-permute-start.6
  278.4 2.4 collective-permute-start.7
  280.9 1.6 collective-permute-start.8
  282.5 28.3 %attention_back.6 = bf16[2048,384]{1,0:T(8,128)(2,1)} custom-call(bf16[2048,384]{1,0:T(8,128)(2,1)} %bitcast.16.mixed_ref.mixed_hbm, bf16[2048,512]{1,0:T(8,128)(2,1)} %get-tuple-element.521.query_hbm, f32[2048,128]{1,0:T(8,128)} %get-tuple-element.522.out_hbm, bf16[2048,128]{1,0:T(8,128)(2,1)} %bitcast.29.grad_hbm), custom_call_target="tpu_custom_call" | custom-call | flops 21474836480 | bytes 6815744 | tf_op jit(solution)/shard_map/attention_back/pallas_call | solution.py:79
  310.8 2.4 collective-permute-done.7.refs_2_
  313.1 4.8 all-to-all-start.18
  323.9 2.8 convert_element_type.79
  326.7 2.8 convert_element_type.82
  329.5 6.2 %all-to-all-done.18.parts_ref.grad_ref = bf16[4,512,384]{2,1,0:T(8,128)(2,1)} async-done(((bf16[4,512,384]{2,1,0:T(8,128)(2,1)}), bf16[4,512,384]{2,1,0:T(8,128)(2,1)}, u32[]{:S(2)}, u32[]{:S(2)}) %all-to-all-start.18) | async-done | bytes 1572896 | tf_op jit(solution)/shard_map/all_to_all | solution.py:966
  335.7 9.8 %middle_back.1 = (bf16[4,512,128]{2,1,0:T(8,128)(2,1)}, f32[512,512]{1,0:T(8,128)}, bf16[512,512]{1,0:T(8,128)(2,1)}, bf16[512,512]{1,0:T(8,128)(2,1)}, bf16[512...) custom-call(s32[1]{0:T(128)} %bitcast.me_ref, bf16[4,512,384]{2,1,0:T(8,128)(2,1)} %all-to-all-done.18.parts_ref.grad_ref, ...), custom_call_target="tpu_custom_call" | custom-call | flops 3221225472 | bytes 19429380 | tf_op jit(solution)/shard_map/middle_back/pallas_call | solution.py:79
  345.5 4.2 all-to-all-start.19
  351.2 8.7 %weight_grads.1 = (bf16[512,1536]{1,0:T(8,128)(2,1)}, bf16[512,2048]{1,0:T(8,128)(2,1)}, bf16[2048,512]{1,0:T(8,128)(2,1)}, bf16[2,512,512]{2,1,0:T(8,128)(2,1)}) custom-call(bf16[512,512]{1,0:T(8,128)(2,1)} %get-tuple-element.544.normed_ref, bf16[4,512,384]{2,1,0:T(8,128)(2,1)} %all-to-all-done.18.parts_ref.grad_ref, ...), custom_call_target="tpu_custom_call" | custom-call | flops 3489660928 | bytes 16252928 | tf_op jit(solution)/shard_map/weight_grads/pallas_call | solution.py:79
  359.9 1.8 broadcast_in_dim.51
  361.6 164.8 %while.18 = (s32[]{:T(128)}, bf16[2816,512]{1,0:T(8,128)(2,1)}, f32[4,128,512]{2,1,0:T(8,128)}, bf16[512,512]{1,0:T(8,128)(2,1)}, s32[]{:T(128)}, /*index=5*/bf1...) while((s32[]{:T(128)}, bf16[2816,512]{1,0:T(8,128)(2,1)}, ...), condition=%wide.wide.region_8.9_spmd, body=%wide.wide.region_4.8_spmd.sunk | while | flops 2819970304 | bytes 95285600 | solution.py:1177
  361.8 25.3 %attention_back.7 = bf16[2048,384]{1,0:T(8,128)(2,1)} custom-call(bf16[2048,384]{1,0:T(8,128)(2,1)} %get-tuple-element.1161.mixed_hbm, bf16[2048,512]{1,0:T(8,128)(2,1)} %get-tuple-element.1162.query_hbm, f32[2048,128]{1,0:T(8,128)} %get-tuple-element.1163.out_hbm, bf16[2048,128]{1,0:T(8,128)(2,1)} %get-tuple-element.1079.grad_hbm), custom_call_target="tpu_custom_call" | custom-call | flops 1 | bytes 6815744 | tf_op jit(solution)/shard_map/while/body/attention_back/pallas_call | solution.py:79
  387.1 4.2 all-to-all-start
  391.6 21.8 %all-to-all-done.parts_ref.grad_ref = bf16[4,512,384]{2,1,0:T(8,128)(2,1)S(1)} async-done(((bf16[4,512,384]{2,1,0:T(8,128)(2,1)}), bf16[4,512,384]{2,1,0:T(8,128)(2,1)S(1)}, u32[]{:S(2)}, u32[]{:S(2)}) %all-to-all-start) | async-done | bytes 1572896 | tf_op jit(solution)/shard_map/while/body/all_to_all | solution.py:966
  414.6 4.6 final_back.5
  420.9 4.4 last_grads.5
  425.3 7.3 %all_to_all.142 = bf16[2,1408,512]{2,1,0:T(8,128)(2,1)S(1)} all-to-all(bf16[2,1408,512]{2,1,0:T(8,128)(2,1)} %bitcast.88), channel_id=1, replica_groups=mesh['dp'=2,'blk'=16] {'dp'}, dimensions={0} | all-to-all | bytes 5767168 | tf_op jit(solution)/shard_map/while/body/all_to_all | solution.py:984
  432.6 2.0 reduce_sum.53
  434.7 23.8 %all_to_all.143 = bf16[4,352,512]{2,1,0:T(8,128)(2,1)S(1)} all-to-all(bf16[4,352,512]{2,1,0:T(8,128)(2,1)} %bitcast.91), channel_id=1, replica_groups={{0,1,2,3},{4,5,6,7},{8,9,10,11},{12,13,14,15},{16,17,18,19},{20,21,22,2..., dimensions={0} | all-to-all | bytes 2883584 | tf_op jit(solution)/shard_map/while/body/all_to_all | solution.py:984
  458.9 19.3 %all_to_all.144 = bf16[4,88,512]{2,1,0:T(8,128)(2,1)S(1)} all-to-all(bf16[4,88,512]{2,1,0:T(8,128)(2,1)S(1)} %bitcast.96), channel_id=1, replica_groups={{0,4,8,12},{1,5,9,13},{2,6,10,14},{3,7,11,15},{16,20,24,28},{17,21,25,2..., dimensions={0} | all-to-all | bytes 720896 | tf_op jit(solution)/shard_map/while/body/all_to_all | solution.py:984
  478.3 11.8 %all_to_all.145 = bf16[4,88,512]{2,1,0:T(8,128)(2,1)S(1)} all-to-all(bf16[4,88,512]{2,1,0:T(8,128)(2,1)S(1)} %broadcast_in_dim.62), channel_id=1, replica_groups={{0,4,8,12},{1,5,9,13},{2,6,10,14},{3,7,11,15},{16,20,24,28},{17,21,25,2..., dimensions={0} | all-to-all | bytes 720896 | tf_op jit(solution)/shard_map/while/body/all_to_all | solution.py:988
  491.3 4.4 all-to-all-start.5
  495.9 1.7 collective-permute-start.1
  497.6 1.8 collective-permute-start.2
  499.5 3.7 combine.5
  503.2 3.6 collective-permute-done.refs_1_
  506.8 3.0 collective-permute-done.1.refs_2_
  509.8 1.9 collective-permute-done.2.refs_3_
  512.3 2.2 gather_pieces.5
  514.5 4.2 all-to-all-done.5
  518.8 7.4 %all_to_all.146 = bf16[2,1408,512]{2,1,0:T(8,128)(2,1)} all-to-all(bf16[2,1408,512]{2,1,0:T(8,128)(2,1)S(1)} %broadcast_in_dim.64), channel_id=1, replica_groups=mesh['dp'=2,'blk'=16] {'dp'}, dimensions={0} | all-to-all | bytes 5767168 | tf_op jit(solution)/shard_map/while/body/all_to_all | solution.py:988
  531.6 9.1 %finish.1 = (f32[512,2048]{1,0:T(8,128)}, f32[2048,512]{1,0:T(8,128)}, f32[2,512,1536]{2,1,0:T(8,128)}, f32[2,512,512]{2,1,0:T(8,128)}) custom-call(bf16[512,2048]{1,0:T(8,128)(2,1)} %get-tuple-element.875.up_ref, bf16[2048,512]{1,0:T(8,128)(2,1)} %get-tuple-element.876.down_ref, bf16[512,1536]{1,0:T(8,128)(2,1)} %get-tuple-element.877.qkv1_ref, ...), custom_call_target="tpu_custom_call" | custom-call | flops 1 | bytes 36962304 | tf_op jit(solution)/shard_map/finish/pallas_call | solution.py:79
  (117 shorter events, 25.0 us)
Async XLA Ops:
  7.2 21.2 %copy-start.10 = (f32[2,512]{1,0:T(2,128)S(1)}, f32[2,512]{1,0:T(2,128)}, u32[]{:S(2)}) copy-start(f32[2,512]{1,0:T(2,128)} %gain_ref.5) | copy-start | bytes 12292
  7.2 21.2 %copy-start.1 = (bf16[2,512,1536]{2,1,0:T(8,128)(2,1)S(1)}, bf16[2,512,1536]{2,1,0:T(8,128)(2,1)}, u32[]{:S(2)}) copy-start(bf16[2,512,1536]{2,1,0:T(8,128)(2,1)} %weight_ref.5) | copy-start | bytes 9437188
  7.2 21.2 %all-to-all-start.7 = ((bf16[4,128,512]{2,1,0:T(8,128)(2,1)}), bf16[4,128,512]{2,1,0:T(8,128)(2,1)}, u32[]{:S(2)}, u32[]{:S(2)}) async-start(bf16[4,128,512]{2,1,0:T(8,128)(2,1)} %param.24), calls=%async_computation.7 | async-start | bytes 1048576 | tf_op jit(solution)/shard_map/all_to_all | solution.py:966
  55.8 18.7 %all-to-all-start.9 = ((bf16[16,72,256]{2,1,0:T(8,128)(2,1)}), bf16[16,72,256]{2,1,0:T(8,128)(2,1)}, u32[]{:S(2)}, u32[]{:S(2)}) async-start(bf16[16,72,256]{2,1,0:T(8,128)(2,1)} %bitcast.109), calls=%async_computation.9 | async-start | bytes 1179648 | tf_op jit(solution)/shard_map/all_to_all | solution.py:966
  85.9 18.6 %all-to-all-start.11 = ((bf16[16,72,256]{2,1,0:T(8,128)(2,1)}), bf16[16,72,256]{2,1,0:T(8,128)(2,1)}, u32[]{:S(2)}, u32[]{:S(2)}) async-start(bf16[16,72,256]{2,1,0:T(8,128)(2,1)} %bitcast.108), calls=%async_computation.11 | async-start | bytes 1179648 | tf_op jit(solution)/shard_map/all_to_all | solution.py:966
  104.5 19.1 %all-to-all-start.12 = ((bf16[4,512,384]{2,1,0:T(8,128)(2,1)}), bf16[4,512,384]{2,1,0:T(8,128)(2,1)}, u32[]{:S(2)}, u32[]{:S(2)}) async-start(bf16[4,512,384]{2,1,0:T(8,128)(2,1)} %get-tuple-element.497), calls=%async_computation.12 | async-start | bytes 3145728 | tf_op jit(solution)/shard_map/all_to_all | solution.py:966
  108.9 28.8 %collective-permute-start.3 = (bf16[128,512]{1,0:T(8,128)(2,1)}, bf16[128,512]{1,0:T(8,128)(2,1)}, u32[]{:S(2)}, u32[]{:S(2)}) collective-permute-start(bf16[128,512]{1,0:T(8,128)(2,1)} %get-tuple-element.500), channel_id=1, source_target_pairs={{0,4},{4,8},{8,12},{12,0},{1,5},{5,9},{9,13},{13,1},{2,6},{6,10},{... | collective-permute-start | bytes 393224 | tf_op jit(solution)/shard_map/ppermute | solution.py:1001
  110.3 27.4 %collective-permute-start.4 = (bf16[128,512]{1,0:T(8,128)(2,1)}, bf16[128,512]{1,0:T(8,128)(2,1)}, u32[]{:S(2)}, u32[]{:S(2)}) collective-permute-start(bf16[128,512]{1,0:T(8,128)(2,1)} %get-tuple-element.501), channel_id=1, source_target_pairs={{0,8},{4,12},{8,0},{12,4},{1,9},{5,13},{9,1},{13,5},{2,10},{6,14},... | collective-permute-start | bytes 393224 | tf_op jit(solution)/shard_map/ppermute | solution.py:1001
  112.1 25.6 %collective-permute-start.5 = (bf16[128,512]{1,0:T(8,128)(2,1)}, bf16[128,512]{1,0:T(8,128)(2,1)}, u32[]{:S(2)}, u32[]{:S(2)}) collective-permute-start(bf16[128,512]{1,0:T(8,128)(2,1)} %get-tuple-element.502), channel_id=1, source_target_pairs={{0,12},{4,0},{8,4},{12,8},{1,13},{5,1},{9,5},{13,9},{2,14},{6,2},{... | collective-permute-start | bytes 393224 | tf_op jit(solution)/shard_map/ppermute | solution.py:1001
  216.6 4.5 copy-start.16
  216.6 5.4 copy-start.14
  216.6 29.9 %all-to-all-start.15 = ((bf16[16,72,512]{2,1,0:T(8,128)(2,1)}), bf16[16,72,512]{2,1,0:T(8,128)(2,1)}, u32[]{:S(2)}, u32[]{:S(2)}) async-start(bf16[16,72,512]{2,1,0:T(8,128)(2,1)} %bitcast.104), calls=%async_computation.15 | async-start | bytes 2359296 | tf_op jit(solution)/shard_map/all_to_all | solution.py:966
  221.0 99.7 %reduce-scatter.15.cloned.1.call-start = ((), (), s32[]{:S(2)}) async-start(), calls=%async_computation.27 | async-start | bytes 196608
  221.9 100.3 %reduce-scatter.13.cloned.1.call-start = ((), (), s32[]{:S(2)}) async-start(), calls=%async_computation.26 | async-start | bytes 786432
  223.1 100.8 %reduce-scatter.9.cloned.1.call-start = ((), (), s32[]{:S(2)}) async-start(), calls=%async_computation.24 | async-start | bytes 3145728 | tf_op jit(solution)/shard_map/reduce_scatter | solution.py:1113
  223.6 7.1 %copy-start.17 = (bf16[1,2048,512]{2,1,0:T(8,128)(2,1)S(1)}, bf16[1,2048,512]{2,1,0:T(8,128)(2,1)}, u32[]{:S(2)}) copy-start(bf16[1,2048,512]{2,1,0:T(8,128)(2,1)} %down_ref.1) | copy-start | bytes 6291460
  223.6 7.1 %copy-start.18 = (f32[1,512]{1,0:T(1,128)S(1)}, f32[1,512]{1,0:T(1,128)}, u32[]{:S(2)}) copy-start(f32[1,512]{1,0:T(1,128)} %down_bias_ref.1) | copy-start | bytes 6148
  223.6 13.3 %slice-start = ((s8[4718592]{0:T(1024)(128)(4,1)}), s8[4194304]{0:T(1024)(128)(4,1)S(1)}, s32[]{:S(2)}) async-start(s8[4718592]{0:T(1024)(128)(4,1)} %bitcast.140), calls=%async_computation.29 | async-start | bytes 8388608
  230.7 6.2 %slice-start.1 = ((s8[4718592]{0:T(1024)(128)(4,1)}), s8[524288]{0:T(1024)(128)(4,1)S(1)}, s32[]{:S(2)}) async-start(s8[4718592]{0:T(1024)(128)(4,1)} %bitcast.140), calls=%async_computation.30 | async-start | bytes 1048576
  230.7 6.2 %copy-start.19 = (bf16[1152,512]{1,0:T(8,128)(2,1)S(1)}, bf16[1152,512]{1,0:T(8,128)(2,1)}, u32[]{:S(2)}) copy-start(bf16[1152,512]{1,0:T(8,128)(2,1)} %get-tuple-element.513) | copy-start | bytes 3538948
  252.2 20.1 %all-to-all-start.16 = ((bf16[16,128,128]{2,1,0:T(8,128)(2,1)}), bf16[16,128,128]{2,1,0:T(8,128)(2,1)}, u32[]{:S(2)}, u32[]{:S(2)}) async-start(bf16[16,128,128]{2,1,0:T(8,128)(2,1)} %get-tuple-element.523), calls=%async_computation.16 | async-start | bytes 1048576 | tf_op jit(solution)/shard_map/all_to_all | solution.py:966
  258.4 68.3 %reduce-scatter.11.cloned.1.call-start = ((), (), s32[]{:S(2)}) async-start(), calls=%async_computation.25 | async-start | bytes 3145728 | tf_op jit(solution)/shard_map/reduce_scatter | solution.py:1113
  272.3 40.9 %all-to-all-start.17 = ((bf16[16,72,512]{2,1,0:T(8,128)(2,1)}), bf16[16,72,512]{2,1,0:T(8,128)(2,1)}, u32[]{:S(2)}, u32[]{:S(2)}) async-start(bf16[16,72,512]{2,1,0:T(8,128)(2,1)} %bitcast.101), calls=%async_computation.17 | async-start | bytes 2359296 | tf_op jit(solution)/shard_map/all_to_all | solution.py:966
  276.7 34.1 %collective-permute-start.6 = (bf16[128,512]{1,0:T(8,128)(2,1)}, bf16[128,512]{1,0:T(8,128)(2,1)}, u32[]{:S(2)}, u32[]{:S(2)}) collective-permute-start(bf16[128,512]{1,0:T(8,128)(2,1)} %get-tuple-element.528), channel_id=1, source_target_pairs={{0,4},{4,8},{8,12},{12,0},{1,5},{5,9},{9,13},{13,1},{2,6},{6,10},{... | collective-permute-start | bytes 393224 | tf_op jit(solution)/shard_map/ppermute | solution.py:1001
  278.4 34.7 %collective-permute-start.7 = (bf16[128,512]{1,0:T(8,128)(2,1)}, bf16[128,512]{1,0:T(8,128)(2,1)}, u32[]{:S(2)}, u32[]{:S(2)}) collective-permute-start(bf16[128,512]{1,0:T(8,128)(2,1)} %get-tuple-element.529), channel_id=1, source_target_pairs={{0,8},{4,12},{8,0},{12,4},{1,9},{5,13},{9,1},{13,5},{2,10},{6,14},... | collective-permute-start | bytes 393224 | tf_op jit(solution)/shard_map/ppermute | solution.py:1001
  280.9 32.3 %collective-permute-start.8 = (bf16[128,512]{1,0:T(8,128)(2,1)}, bf16[128,512]{1,0:T(8,128)(2,1)}, u32[]{:S(2)}, u32[]{:S(2)}) collective-permute-start(bf16[128,512]{1,0:T(8,128)(2,1)} %get-tuple-element.530), channel_id=1, source_target_pairs={{0,12},{4,0},{8,4},{12,8},{1,13},{5,1},{9,5},{13,9},{2,14},{6,2},{... | collective-permute-start | bytes 393224 | tf_op jit(solution)/shard_map/ppermute | solution.py:1001
  310.7 8.4 %copy-start.13 = (f32[16,2]{1,0:T(8,128)S(1)}, f32[16,2]{1,0:T(8,128)}, u32[]{:S(2)}) copy-start(f32[16,2]{1,0:T(8,128)} %get-tuple-element.562) | copy-start | bytes 388
  310.7 8.4 %copy-start.15 = (s32[4,128,2]{1,2,0:T(2,128)S(1)}, s32[4,128,2]{1,2,0:T(2,128)}, u32[]{:S(2)}) copy-start(s32[4,128,2]{1,2,0:T(2,128)} %param.44) | copy-start | bytes 12292
  313.1 22.6 %all-to-all-start.18 = ((bf16[4,512,384]{2,1,0:T(8,128)(2,1)}), bf16[4,512,384]{2,1,0:T(8,128)(2,1)}, u32[]{:S(2)}, u32[]{:S(2)}) async-start(bf16[4,512,384]{2,1,0:T(8,128)(2,1)} %bitcast.100), calls=%async_computation.18 | async-start | bytes 3145728 | tf_op jit(solution)/shard_map/all_to_all | solution.py:966
  335.7 14.0 %copy-start.11 = (f32[16,512]{1,0:T(8,128)S(1)}, f32[16,512]{1,0:T(8,128)}, u32[]{:S(2)}) copy-start(f32[16,512]{1,0:T(8,128)} %get-tuple-element.834) | copy-start | bytes 98308
  335.7 14.0 %copy-start.12 = (f32[8,512]{1,0:T(8,128)S(1)}, f32[8,512]{1,0:T(8,128)}, u32[]{:S(2)}) copy-start(f32[8,512]{1,0:T(8,128)} %get-tuple-element.826) | copy-start | bytes 49156
  345.5 14.4 %all-to-all-start.19 = ((bf16[4,512,128]{2,1,0:T(8,128)(2,1)}), bf16[4,512,128]{2,1,0:T(8,128)(2,1)}, u32[]{:S(2)}, u32[]{:S(2)}) async-start(bf16[4,512,128]{2,1,0:T(8,128)(2,1)} %get-tuple-element.543), calls=%async_computation.21 | async-start | bytes 1048576 | tf_op jit(solution)/shard_map/all_to_all | solution.py:966
  349.6 182.0 %all-reduce.5.cloned.1.call-start = ((), (), s32[]{:S(2)}) async-start(), calls=%async_computation.28 | async-start | bytes 11534336 | tf_op jit(solution)/shard_map/psum | solution.py:1143
  387.1 27.5 %copy-start.3 = (f32[512,512]{1,0:T(8,128)S(1)}, f32[512,512]{1,0:T(8,128)}, u32[]{:S(2)}) copy-start(f32[512,512]{1,0:T(8,128)} %get-tuple-element.1167.first_grad_ref) | copy-start | bytes 3145732 | tf_op jit(solution)/shard_map/while
  387.1 26.3 %all-to-all-start = ((bf16[4,512,384]{2,1,0:T(8,128)(2,1)}), bf16[4,512,384]{2,1,0:T(8,128)(2,1)S(1)}, u32[]{:S(2)}, u32[]{:S(2)}) async-start(bf16[4,512,384]{2,1,0:T(8,128)(2,1)} %bitcast.89), calls=%async_computation | async-start | bytes 3145728 | tf_op jit(solution)/shard_map/while/body/all_to_all | solution.py:966
  413.4 1.1 copy-start
  414.6 6.4 %copy-start.4 = (bf16[512,512]{1,0:T(8,128)(2,1)S(1)}, bf16[512,512]{1,0:T(8,128)(2,1)}, u32[]{:S(2)}) copy-start(bf16[512,512]{1,0:T(8,128)(2,1)} %get-tuple-element.1174.normed_ref) | copy-start | bytes 1572868 | tf_op jit(solution)/shard_map/while
  490.1 9.4 %copy-start.8 = (f32[512,512]{1,0:T(8,128)S(1)}, f32[512,512]{1,0:T(8,128)}, u32[]{:S(2)}) copy-start(f32[512,512]{1,0:T(8,128)} %get-tuple-element.1178.upper_ref) | copy-start | bytes 3145732 | tf_op jit(solution)/shard_map/while
  490.1 9.4 %copy-start.9 = (s32[512,2]{1,0:T(8,128)S(1)}, s32[512,2]{1,0:T(8,128)}, u32[]{:S(2)}) copy-start(s32[512,2]{1,0:T(8,128)} %get-tuple-element.1176.choice_ref) | copy-start | bytes 12292 | tf_op jit(solution)/shard_map/while
  491.3 27.4 %all-to-all-start.5 = ((bf16[4,352,512]{2,1,0:T(8,128)(2,1)}), bf16[4,352,512]{2,1,0:T(8,128)(2,1)S(1)}, u32[]{:S(2)}, u32[]{:S(2)}) async-start(bf16[4,352,512]{2,1,0:T(8,128)(2,1)} %broadcast_in_dim.63), calls=%async_computation.5 | async-start | bytes 2883584 | tf_op jit(solution)/shard_map/while/body/all_to_all | solution.py:988
  495.6 11.2 %collective-permute-start = (bf16[128,512]{1,0:T(8,128)(2,1)}, bf16[128,512]{1,0:T(8,128)(2,1)S(1)}, u32[]{:S(2)}, u32[]{:S(2)}) collective-permute-start(bf16[128,512]{1,0:T(8,128)(2,1)} %get-tuple-element.1083), channel_id=1, source_target_pairs={{0,4},{4,8},{8,12},{12,0},{1,5},{5,9},{9,13},{13,1},{2,6},{6,10},{... | collective-permute-start | bytes 393224 | tf_op jit(solution)/shard_map/while/body/ppermute | solution.py:1001
  495.9 13.8 %collective-permute-start.1 = (bf16[128,512]{1,0:T(8,128)(2,1)}, bf16[128,512]{1,0:T(8,128)(2,1)S(1)}, u32[]{:S(2)}, u32[]{:S(2)}) collective-permute-start(bf16[128,512]{1,0:T(8,128)(2,1)} %get-tuple-element.1084), channel_id=1, source_target_pairs={{0,8},{4,12},{8,0},{12,4},{1,9},{5,13},{9,1},{13,5},{2,10},{6,14},... | collective-permute-start | bytes 393224 | tf_op jit(solution)/shard_map/while/body/ppermute | solution.py:1001
  497.6 14.0 %collective-permute-start.2 = (bf16[128,512]{1,0:T(8,128)(2,1)}, bf16[128,512]{1,0:T(8,128)(2,1)S(1)}, u32[]{:S(2)}, u32[]{:S(2)}) collective-permute-start(bf16[128,512]{1,0:T(8,128)(2,1)} %get-tuple-element.1085), channel_id=1, source_target_pairs={{0,12},{4,0},{8,4},{12,8},{1,13},{5,1},{9,5},{13,9},{2,14},{6,2},{... | collective-permute-start | bytes 393224 | tf_op jit(solution)/shard_map/while/body/ppermute | solution.py:1001
  506.8 4.9 copy-start.5
  509.8 1.9 copy-start.6
  511.6 0.7 copy-start.7
  518.8 7.4 %copy-start.2 = (bf16[2,512,1536]{2,1,0:T(8,128)(2,1)S(1)}, bf16[2,512,1536]{2,1,0:T(8,128)(2,1)}, u32[]{:S(2)}) copy-start(bf16[2,512,1536]{2,1,0:T(8,128)(2,1)} %get-tuple-element.1232) | copy-start | bytes 9437188 | tf_op jit(solution)/shard_map/while
Sparse Core Ops, SparseCore 0:
  224.1 8.6 reduce-scatter.14
  235.1 9.1 reduce-scatter.12
  247.1 10.7 reduce-scatter.8
  261.8 10.8 reduce-scatter.10
  360.0 171.5 all-reduce.4
